TPU v7x, 32 devices: a whole 2x2x4 slice. The times are simulated.
32 devices in a mesh: batch: 4 (over y, x), dir: 8 (over z, core).
Axes of the slice: x: 2, y: 2, z: 4, core: 2. Of those that a mesh axis runs over, the one named last changes fastest.
Arguments:
- embeddings: bfloat16 [128, 2048], P(('batch', 'dir')), may hold values from -13 to 13
- directions: bfloat16 [2048, 2048], P(None, 'dir'), may hold values from -0.125 to 0.125
Outputs:
- grad_embed: float32 [128, 2048], P(('batch', 'dir'))
All inputs are finite; a program needn't handle non-finite values.
Results may differ from a plain program's by a relative error of at most 0.0016.
Values may be sent and summed in bfloat16 or wider, within the bound.
A program may use at most 64 MiB of HBM per device.

v0:
```python
import jax
import jax.numpy as jnp
from jax import lax
from jax.sharding import PartitionSpec as P

KNOTS = 17


def knot_table():
    index = jnp.arange(KNOTS, dtype=jnp.float32)
    spacing = 3.0 / (KNOTS - 1)
    knot_pos = index * spacing
    target = jnp.exp(-0.5 * knot_pos * knot_pos)
    ends = jnp.where((index == 0) | (index == KNOTS - 1), 0.5, 1.0)
    weights = ends * spacing * target
    return (knot_pos, weights, target)


def local(embeddings, directions):
    dir_float = directions.astype(jnp.float32)
    unit = (
        dir_float / jnp.sqrt(jnp.sum(dir_float * dir_float, axis=0, keepdims=True) + 1e-06)
    ).astype(jnp.bfloat16)
    projected = jnp.dot(
        lax.all_gather(embeddings, "dir", axis=0, tiled=True),
        unit,
        preferred_element_type=jnp.float32,
    )
    total_rows = embeddings.shape[0] * lax.axis_size("dir") * lax.axis_size("batch")
    knot_pos, weights, target = knot_table()
    angles = knot_pos[:, None, None] * projected[None]
    cosine_vals = jnp.cos(angles)
    sine_vals = jnp.sin(angles)
    cos_part = jnp.sum(cosine_vals, axis=1)
    sin_part = jnp.sum(sine_vals, axis=1)
    cos_total, sin_total = lax.psum((cos_part, sin_part), "batch")
    cos_mean = cos_total / total_rows
    sin_mean = sin_total / total_rows
    cos_coef = 2.0 * weights[:, None] * (cos_mean - target[:, None])
    sin_coef = 2.0 * weights[:, None] * sin_mean
    grad_proj = jnp.sum(
        knot_pos[:, None, None]
        * (cosine_vals * sin_coef[:, None, :] - sine_vals * cos_coef[:, None, :]),
        axis=0,
    ).astype(jnp.bfloat16)
    return lax.psum_scatter(
        lax.dot_general(
            grad_proj, unit, (((1,), (1,)), ((), ())), preferred_element_type=jnp.float32
        ),
        "dir",
        scatter_dimension=0,
        tiled=True,
    )


def solution(mesh):
    placed = (P(("batch", "dir"), None), P(None, "dir"))
    return jax.shard_map(
        local, mesh=mesh, in_specs=placed, out_specs=P(("batch", "dir"), None), check_vma=False
    )
```

profile of v0, /device:TPU:0, one launch (start us, length us, event | category | flops | bytes accessed | tf_op | source)
XLA Modules:
  0.0 109.7 jit_solution(17829690845782955907)
XLA Ops:
  6.5 0.0 copy-start
  6.5 0.0 all-reduce.4.cloned.1.call-start
  6.6 1.6 %fusion = f32[256]{0:T(256)S(1)} fusion(bf16[2048,256]{1,0:T(8,128)(2,1)} %param.3), kind=kLoop, calls=%fused_computation.2 | loop fusion | flops 1572608 | bytes 1049600 | tf_op jit(solution)/shard_map/reduce_sum | solution.py:22
  8.2 0.0 copy-done
  8.2 0.0 copy-start.1
  8.2 0.2 fusion.1
  8.4 0.5 copy-done.1
  8.9 15.7 %all-gather = bf16[8,4,2048]{2,1,0:T(4,128)(2,1)S(1)} all-gather(bf16[1,4,2048]{2,1,0:T(4,128)(2,1)S(1)} %bitcast.8), channel_id=1, replica_groups=mesh['batch'=4,'dir'=8] {'dir'}, dimensions={0}, use_global_device_ids=true | all-gather | bytes 147456 | tf_op jit(solution)/shard_map/all_gather | solution.py:25
  24.7 0.3 convolution_bitcast_fusion
  25.0 2.2 %fusion.5 = (f32[17,256]{1,0:T(8,128)S(1)}, f32[17,256]{1,0:T(8,128)S(1)}) fusion(f32[32,256]{1,0:T(8,128)S(1)} %convolution_bitcast_fusion, f32[17]{0:T(128)S(1)} %iota_multiply_fusion.1), kind=kLoop, calls=%fused_computation.10 | loop fusion | flops 409088 | bytes 67652 | tf_op jit(solution)/shard_map/reduce_sum | solution.py:35
  27.1 16.7 %all-reduce.1 = (f32[17,256]{1,0:T(8,128)S(1)}, f32[17,256]{1,0:T(8,128)S(1)}) all-reduce(f32[17,256]{1,0:T(8,128)S(1)} %get-tuple-element.6, f32[17,256]{1,0:T(8,128)S(1)} %get-tuple-element.5), channel_id=1, replica_groups=mesh['batch'=4,'dir'=8] {'batch'}, use_global_device_ids=true, to_apply=%region_4.5 | all-reduce | flops 8704 | bytes 69632 | tf_op jit(solution)/shard_map/psum | solution.py:36
  43.9 0.1 subtract_multiply_fusion
  44.0 0.0 copy-start.2
  44.0 2.1 %fusion.8 = bf16[32,256]{1,0:T(8,128)(2,1)S(1)} fusion(f32[17,256]{1,0:T(8,128)S(1)} %get-tuple-element.9, f32[17,256]{1,0:T(8,128)S(1)} %get-tuple-element.10, f32[32,256]{1,0:T(8,128)S(1)} %convolution_bitcast_fusion, f32[17]{0:T(128)S(1)} %iota_multiply_fusion.1), kind=kLoop, calls=%fused_computation.13 | loop fusion | flops 827392 | bytes 84036 | tf_op jit(solution)/shard_map/reduce_sum | solution.py:41
  46.1 1.1 %fusion.15 = f32[32,2048]{1,0:T(8,128)} fusion(bf16[32,256]{1,0:T(8,128)(2,1)S(1)} %fusion.8, bf16[2048,256]{1,0:T(8,128)(2,1)S(1)} %fusion.1), kind=kOutput, calls=%fused_computation.29 | convolution fusion | flops 33554432 | bytes 1327104 | tf_op jit(solution)/shard_map/dot_general | solution.py:47
  47.2 0.0 all-reduce.4.cloned.1.call-update
  47.2 0.0 copy-done.2
  47.2 0.6 dynamic-slice
  48.4 53.0 %all-reduce.4.cloned.1.call-done = f32[32,2048]{1,0:T(8,128)} async-done(((f32[32,2048]{1,0:T(8,128)}), f32[32,2048]{1,0:T(8,128)}) %all-reduce.4.cloned.1.call-update) | async-done | bytes 262160
  101.4 1.5 %constant_dynamic-slice_fusion = f32[4,2048]{1,0:T(4,128)} fusion(f32[32,2048]{1,0:T(8,128)} %all-reduce.4.cloned.1.call-done, u32[]{:T(128)S(6)} %multiply.9), kind=kLoop, calls=%fused_computation.25 | loop fusion | bytes 65540
  (6 shorter events, 0.1 us)
Async XLA Ops:
  6.5 1.7 %copy-start = (bf16[2048,256]{1,0:T(8,128)(2,1)S(1)}, bf16[2048,256]{1,0:T(8,128)(2,1)}, u32[]{:S(2)}) copy-start(bf16[2048,256]{1,0:T(8,128)(2,1)} %param.3) | copy-start | bytes 3145732
  6.5 94.9 %all-reduce.4.cloned.1.call-start = ((), (), s32[]{:S(2)}) async-start(), calls=%async_computation | async-start | bytes 524288
  8.2 0.7 copy-start.1
  44.0 3.3 %copy-start.2 = (u32[32]{0:T(128)S(1)}, u32[32]{0:T(128)}, u32[]{:S(2)}) copy-start(u32[32]{0:T(128)} %constant.27) | copy-start | bytes 388
Sparse Core Ops, SparseCore 0:
  47.3 54.0 all-reduce.3
where the time goes:
time: 110 us
  waiting for transfers between devices  53 us (48%)
  blocking collectives  32.4 us (29%)
  between operations  14.1 us (13%)
  other arithmetic  6.22 us (6%)
  local copies, waits for them, and re-layouts  2.59 us (2%)
  matrix products  1.4 us (1%)
    unnamed x2, waiting for transfers between devices  53 us
    psum x1, blocking collectives, local(): cos_total, sin_total = lax.psum((cos_part, sin_part), 'batch')  16.7 us
    all_gather x1, blocking collectives, local(): lax.all_gather(embeddings, 'dir', axis=0, tiled=True)  15.7 us
    unnamed x9, local copies, waits for them, and re-layouts  2.59 us
  transfers between devices with their start and end apart: 1, of which 1 were waited for; matrix products, arithmetic and copies ran while one was open for 1% of the time, Pallas kernels for 0%

commit v1 on v0

v1 whole, which is shorter than its diff:
```python
import functools

import jax
import jax.numpy as jnp
from jax import lax
from jax.experimental import pallas as pl
from jax.experimental.pallas import tpu as pltpu
from jax.sharding import PartitionSpec as P

KNOTS = 17
SPACING = 3.0 / (KNOTS - 1)
MESH = pl.DeviceIdType.MESH
TILE = 16
PARTS = 4
STEPS = 8


def sin_cos(angle):
    n = jnp.round(angle * 0.15915494309189535)
    rest = ((angle - n * 6.28125) - n * 1.9350051879882812e-3) - n * 3.019915981956753e-7
    rest = rest * 0.25
    z = rest * rest
    sine = rest + rest * z * (-1.6666654611e-1 + z * (8.3321608736e-3 - z * 1.9515295891e-4))
    cosine = 1.0 - 0.5 * z + z * z * (
        4.166664568298827e-2 + z * (-1.388731625493765e-3 + z * 2.443315711809948e-5)
    )
    for _ in range(2):
        twice = sine + sine
        sine, cosine = twice * cosine, 1.0 - twice * sine
    return sine, cosine


def kernel(
    nb, nd, emb_ref, dir_ref, out_ref,
    raw, unit, blocks, rows_f32, waves, acc, sums, coef,
    pair_out, pair_in, z_out, z_in,
    raw_sem, own_sem, e_send, e_recv, f_send, s_send, s_recv, p_send, p_recv, z_send, z_recv,
):
    chips = nd // 2
    half = chips * emb_ref.shape[0]
    per = emb_ref.shape[0]
    depth = raw.shape[0]
    total_rows = half * 2 * nb
    b, d = lax.axis_index("batch"), lax.axis_index("dir")
    chip, core = d // 2, lax.rem(d, 2)
    other = 1 - core
    partner = (b, chip * 2 + other)
    step_rows = depth // STEPS

    loads = []
    for i in range(STEPS):
        part = pl.ds(i * step_rows, step_rows)
        load = pltpu.make_async_copy(dir_ref.at[part], raw.at[part], raw_sem.at[i])
        load.start()
        loads.append(load)
    own = pltpu.make_async_copy(emb_ref, blocks.at[d], own_sem)
    own.start()

    chip_peers = [lax.rem(chip + j, chips) for j in range(1, chips)]
    batch_peers = [lax.rem(b + j, nb) for j in range(1, nb)]
    barrier = pltpu.get_barrier_semaphore()
    for c in chip_peers:
        pl.semaphore_signal(barrier, inc=1, device_id=(b, c * 2 + core), device_id_type=MESH)
    for a in batch_peers:
        pl.semaphore_signal(barrier, inc=1, device_id=(a, d), device_id_type=MESH)
    pl.semaphore_signal(barrier, inc=1, device_id=partner, device_id_type=MESH)
    pl.semaphore_wait(barrier, len(chip_peers) + len(batch_peers) + 1)

    def send_block(src, slot, sem, device):
        return pltpu.make_async_remote_copy(
            src_ref=src, dst_ref=blocks.at[slot], send_sem=sem, recv_sem=e_recv.at[slot],
            device_id=device, device_id_type=MESH,
        )

    sent = []
    for j, c in enumerate(chip_peers):
        copy = send_block(emb_ref, d, e_send.at[j], (b, c * 2 + core))
        copy.start()
        sent.append(copy)
    copy = send_block(emb_ref, d, e_send.at[chips - 1], partner)
    copy.start()
    sent.append(copy)

    square = jnp.zeros((8, raw.shape[1]), jnp.float32)
    for i in range(STEPS):
        loads[i].wait()
        value = raw[pl.ds(i * step_rows, step_rows), :].astype(jnp.float32)
        square = square + jnp.sum((value * value).reshape(step_rows // 8, 8, -1), axis=0)
    scale = 1.0 / jnp.sqrt(jnp.sum(square, axis=0, keepdims=True) + 1e-06)
    for i in range(STEPS):
        part = pl.ds(i * step_rows, step_rows)
        unit[part, :] = (raw[part, :].astype(jnp.float32) * scale).astype(jnp.bfloat16)

    own.wait()
    for j, c in enumerate(chip_peers):
        slot = c * 2 + core
        send_block(emb_ref, slot, e_send.at[j], partner).wait_recv()
        copy = send_block(blocks.at[slot], slot, f_send.at[j], partner)
        copy.start()
        sent.append(copy)

    def project(which, side):
        for c in range(chips):
            rows_f32[which, c * per:(c + 1) * per, :] = blocks[c * 2 + side].astype(jnp.float32)
        return jnp.dot(
            rows_f32[which].astype(jnp.bfloat16), unit[...], preferred_element_type=jnp.float32
        )

    def fold(value):
        return jnp.sum(value.reshape(TILE // 8, 8, -1), axis=0)

    def trig(which, projected):
        for r in range(half // TILE):
            first = which == 0 and r == 0
            at = which * half + r * TILE
            sine1, cosine1 = sin_cos(SPACING * projected[r * TILE:(r + 1) * TILE])
            powers = {1: (cosine1, sine1)}
            for k in range(1, KNOTS):
                if k > 1 and k % 2 == 0:
                    cosine, sine = powers[k // 2]
                    twice = cosine + cosine
                    powers[k] = (twice * cosine - 1.0, twice * sine)
                elif k > 1:
                    cosine, sine = powers[k - 1]
                    powers[k] = (
                        cosine * cosine1 - sine * sine1, sine * cosine1 + cosine * sine1
                    )
                for s in range(2):
                    waves[k - 1, s, at:at + TILE, :] = powers[k][s]
                    part = fold(powers[k][s])
                    acc[s, k - 1] = part if first else acc[s, k - 1] + part

    trig(0, project(0, core))
    send_rest = [lax.rem(chip + j, chips) * 2 + other for j in range(chips)]
    for slot in send_rest:
        send_block(emb_ref, slot, e_send.at[0], partner).wait_recv()
    trig(1, project(1, other))

    knots = KNOTS - 1
    for s in range(2):
        sums[b, s * knots:(s + 1) * knots, :] = jnp.sum(acc[s], axis=1)
    mine = sums.at[b]
    for j, a in enumerate(batch_peers):
        copy = pltpu.make_async_remote_copy(
            src_ref=mine, dst_ref=sums.at[b], send_sem=s_send.at[j], recv_sem=s_recv.at[b],
            device_id=(a, d), device_id_type=MESH,
        )
        copy.start()
        sent.append(copy)
    width = raw.shape[1]
    knot = lax.broadcasted_iota(jnp.int32, (knots, width), 0).astype(jnp.float32) + 1.0
    pos = knot * SPACING
    target = jnp.exp(-0.5 * pos * pos)
    ends = jnp.where(knot == float(knots), 0.5, 1.0)
    weight = 2.0 * (ends * SPACING * target)
    for j, a in enumerate(batch_peers):
        pltpu.make_async_remote_copy(
            src_ref=mine, dst_ref=sums.at[a], send_sem=s_send.at[j], recv_sem=s_recv.at[a],
            device_id=(a, d), device_id_type=MESH,
        ).wait_recv()
    total = sums[0]
    for a in range(1, nb):
        total = total + sums[a]
    mean = total * (1.0 / total_rows)
    coef[0:knots, :] = pos * (weight * (mean[0:knots] - target))
    coef[knots:2 * knots, :] = pos * (weight * mean[knots:2 * knots])
    ones = jnp.full((1, width), 1.0, jnp.float32)
    zeros = jnp.zeros((1, width), jnp.float32)
    end = 2.0 * 0.5 * SPACING
    first_term = 0.0 * (ones * (end * zeros) - zeros * (end * (ones - 1.0)))

    def grad(which):
        tiles = []
        for r in range(half // TILE):
            at = which * half + r * TILE
            value = jnp.broadcast_to(first_term, (TILE, width))
            for k in range(knots):
                value = value + (
                    waves[k, 0, at:at + TILE, :] * coef[knots + k:knots + k + 1, :]
                    - waves[k, 1, at:at + TILE, :] * coef[k:k + 1, :]
                )
            tiles.append(value)
        value = tiles[0] if len(tiles) == 1 else jnp.concatenate(tiles, axis=0)
        return value.astype(jnp.bfloat16)

    columns = depth // PARTS

    def back(value, p):
        return lax.dot_general(
            value, unit[p * columns:(p + 1) * columns, :], (((1,), (1,)), ((), ())),
            preferred_element_type=jnp.float32,
        )

    away = grad(1)
    pairs = []
    for p in range(PARTS):
        pair_out[p] = back(away, p)
        copy = pltpu.make_async_remote_copy(
            src_ref=pair_out.at[p], dst_ref=pair_in.at[p], send_sem=p_send.at[p],
            recv_sem=p_recv.at[p], device_id=partner, device_id_type=MESH,
        )
        copy.start()
        pairs.append(copy)
        sent.append(copy)
    home = grad(0)
    for p in range(PARTS):
        value = back(home, p)
        pairs[p].wait_recv()
        value = value + pair_in[p]
        for c in range(chips):
            z_out[p, c] = value[c * per:(c + 1) * per]
        for j, c in enumerate(chip_peers):
            copy = pltpu.make_async_remote_copy(
                src_ref=z_out.at[p, c], dst_ref=z_in.at[p, chip], send_sem=z_send.at[p, j],
                recv_sem=z_recv.at[p, chip], device_id=(b, c * 2 + core), device_id_type=MESH,
            )
            copy.start()
            sent.append(copy)
    for p in range(PARTS):
        value = z_out[p, chip]
        for j, c in enumerate(chip_peers):
            pltpu.make_async_remote_copy(
                src_ref=z_out.at[p, c], dst_ref=z_in.at[p, c], send_sem=z_send.at[p, j],
                recv_sem=z_recv.at[p, c], device_id=(b, c * 2 + core), device_id_type=MESH,
            ).wait_recv()
            value = value + z_in[p, c]
        out_ref[:, p * columns:(p + 1) * columns] = value
    for copy in sent:
        copy.wait_send()


def local(nb, nd, embeddings, directions):
    per, depth = embeddings.shape
    width = directions.shape[1]
    chips = nd // 2
    half = chips * per
    knots = KNOTS - 1
    columns = depth // PARTS
    f32, bf16 = jnp.float32, jnp.bfloat16
    dma = pltpu.SemaphoreType.DMA
    return pl.pallas_call(
        functools.partial(kernel, nb, nd),
        out_shape=jax.ShapeDtypeStruct((per, depth), f32),
        in_specs=[pl.BlockSpec(memory_space=pl.ANY)] * 2,
        out_specs=pl.BlockSpec(memory_space=pltpu.VMEM),
        scratch_shapes=[
            pltpu.VMEM((depth, width), bf16),
            pltpu.VMEM((depth, width), bf16),
            pltpu.VMEM((nd, per, depth), bf16),
            pltpu.VMEM((2, half, depth), f32),
            pltpu.VMEM((knots, 2, 2 * half, width), f32),
            pltpu.VMEM((2, knots, 8, width), f32),
            pltpu.VMEM((nb, 2 * knots, width), f32),
            pltpu.VMEM((2 * knots, width), f32),
            pltpu.VMEM((PARTS, half, columns), f32),
            pltpu.VMEM((PARTS, half, columns), f32),
            pltpu.VMEM((PARTS, chips, per, columns), f32),
            pltpu.VMEM((PARTS, chips, per, columns), f32),
            dma((STEPS,)),
            dma,
            dma((chips,)),
            dma((nd,)),
            dma((chips,)),
            dma((nb,)),
            dma((nb,)),
            dma((PARTS,)),
            dma((PARTS,)),
            dma((PARTS, chips)),
            dma((PARTS, chips)),
        ],
        compiler_params=pltpu.CompilerParams(
            collective_id=0, has_side_effects=True, vmem_limit_bytes=48 * 1024 * 1024
        ),
        name="sigreg_backward",
    )(embeddings, directions)


def solution(mesh):
    placed = (P(("batch", "dir"), None), P(None, "dir"))
    return jax.shard_map(
        functools.partial(local, mesh.shape["batch"], mesh.shape["dir"]),
        mesh=mesh, in_specs=placed, out_specs=P(("batch", "dir"), None), check_vma=False,
    )
```

time: 110 us -> 25.8 us (0.23)
  waiting for transfers between devices: 53 us -> 0 us
  blocking collectives: 32.4 us -> 0 us
  Pallas kernels: 0 us -> 23 us
  between operations: 14.1 us -> 0.01 us
  other arithmetic: 6.22 us -> 0 us
  matrix products: 1.4 us -> 0 us
    unnamed x2 -> x0, waiting for transfers between devices: 53 us -> none
    pallas_call x0 -> x1, Pallas kernels: none -> 23 us  [local(): pl.pallas_call(functools.partial(kernel, nb, nd), out_shape=jax.ShapeDtyp...]
    psum x1 -> x0, blocking collectives: 16.7 us -> none  [local(): cos_total, sin_total = lax.psum((cos_part, sin_part), 'batch')]
    all_gather x1 -> x0, blocking collectives: 15.7 us -> none  [local(): lax.all_gather(embeddings, 'dir', axis=0, tiled=True)]
    reduce_sum x3 -> x0, other arithmetic: 5.89 us -> none  [the longest x1 2.18 us: local(): sin_part = jnp.sum(sine_vals, axis=1)]
    dot_general x2 -> x0, matrix products: 1.4 us -> none  [the longest x1 1.12 us: local(): lax.dot_general(grad_proj, unit, (((1,), (1,)), ((), ())), preferred_elem...]
    unnamed x9 -> x5, local copies, waits for them, and re-layouts: 2.59 us -> 2.56 us
  transfers between devices with their start and end apart: 1 -> 0, of which waited for: 1 -> 0; matrix products, arithmetic and copies ran while one was open for 1% -> 0% of each run, Pallas kernels for 0% -> 0%
where the time goes in v1:
time: 25.8 us; the launch traced here: 25.5 us
  Pallas kernels  23 us (89%)
  local copies, waits for them, and re-layouts  2.56 us (10%)
    pallas_call x1, Pallas kernels, local(): pl.pallas_call(functools.partial(kernel, nb, nd), out_shape=jax.ShapeDtyp...  23 us
    unnamed x5, local copies, waits for them, and re-layouts  2.56 us

profile of v1, /device:TPU:0, one launch (start us, length us, event | category | flops | bytes accessed | tf_op | source)
XLA Modules:
  0.0 25.5 jit_solution(17754188288563383932)
XLA Ops:
  0.0 0.0 copy-start
  0.0 1.2 %copy-done = bf16[2048,256]{1,0:T(8,128)(2,1)S(1)} copy-done((bf16[2048,256]{1,0:T(8,128)(2,1)S(1)}, bf16[2048,256]{1,0:T(8,128)(2,1)}, u32[]{:S(2)}) %copy-start) | copy-done | bytes 1048600
  1.2 0.0 copy-start.1
  1.2 0.7 %copy-done.1 = bf16[4,2048]{1,0:T(4,128)(2,1)S(1)} copy-done((bf16[4,2048]{1,0:T(4,128)(2,1)S(1)}, bf16[4,2048]{1,0:T(4,128)(2,1)}, u32[]{:S(2)}) %copy-start.1) | copy-done | bytes 16408
  1.9 23.0 %sigreg_backward.1 = f32[4,2048]{1,0:T(4,128)S(1)} custom-call(bf16[4,2048]{1,0:T(4,128)(2,1)S(1)} %copy-done.1, bf16[2048,256]{1,0:T(8,128)(2,1)S(1)} %copy-done), custom_call_target="tpu_custom_call" | custom-call | tf_op jit(solution)/shard_map/sigreg_backward/pallas_call | solution.py:241
  24.9 0.6 %copy.4 = f32[4,2048]{1,0:T(4,128)} copy(f32[4,2048]{1,0:T(4,128)S(1)} %sigreg_backward.1) | data formatting | bytes 65536
Async XLA Ops:
  0.0 1.2 %copy-start = (bf16[2048,256]{1,0:T(8,128)(2,1)S(1)}, bf16[2048,256]{1,0:T(8,128)(2,1)}, u32[]{:S(2)}) copy-start(bf16[2048,256]{1,0:T(8,128)(2,1)} %dir_ref.1) | copy-start | bytes 3145732
  1.2 0.7 %copy-start.1 = (bf16[4,2048]{1,0:T(4,128)(2,1)S(1)}, bf16[4,2048]{1,0:T(4,128)(2,1)}, u32[]{:S(2)}) copy-start(bf16[4,2048]{1,0:T(4,128)(2,1)} %emb_ref.1) | copy-start | bytes 49156

commit v2 on v1

--- a/solution.py
+++ b/solution.py
@@ -13,6 +13,17 @@
 TILE = 16
 PARTS = 4
 STEPS = 8
+LIFT = 2.0 ** 50
+
+
+def to_wire(value):
+    value = value * LIFT
+    return (value * jnp.abs(value)).astype(jnp.bfloat16)
+
+
+def from_wire(value):
+    value = value.astype(jnp.float32)
+    return value * lax.rsqrt(jnp.maximum(jnp.abs(value), 2.0 ** -126)) * (1.0 / LIFT)
 
 
 def sin_cos(angle):
@@ -33,7 +44,7 @@
 def kernel(
     nb, nd, emb_ref, dir_ref, out_ref,
     raw, unit, blocks, rows_f32, waves, acc, sums, coef,
-    pair_out, pair_in, z_out, z_in,
+    pair_out, pair_in, z_own, z_out, z_in,
     raw_sem, own_sem, e_send, e_recv, f_send, s_send, s_recv, p_send, p_recv, z_send, z_recv,
 ):
     chips = nd // 2
@@ -73,25 +84,34 @@
         )
 
     sent = []
+    own.wait()
     for j, c in enumerate(chip_peers):
-        copy = send_block(emb_ref, d, e_send.at[j], (b, c * 2 + core))
+        copy = send_block(blocks.at[d], d, e_send.at[j], (b, c * 2 + core))
         copy.start()
         sent.append(copy)
-    copy = send_block(emb_ref, d, e_send.at[chips - 1], partner)
+    copy = send_block(blocks.at[d], d, e_send.at[chips - 1], partner)
     copy.start()
     sent.append(copy)
 
-    square = jnp.zeros((8, raw.shape[1]), jnp.float32)
-    for i in range(STEPS):
-        loads[i].wait()
-        value = raw[pl.ds(i * step_rows, step_rows), :].astype(jnp.float32)
-        square = square + jnp.sum((value * value).reshape(step_rows // 8, 8, -1), axis=0)
+    for load in loads:
+        load.wait()
+    width = raw.shape[1]
+
+    def add_squares(i, square):
+        part = pl.ds(pl.multiple_of(i * step_rows, step_rows), step_rows)
+        value = raw[part, :].astype(jnp.float32)
+        return square + jnp.sum((value * value).reshape(step_rows // 8, 8, width), axis=0)
+
+    square = lax.fori_loop(0, STEPS, add_squares, jnp.zeros((8, width), jnp.float32))
     scale = 1.0 / jnp.sqrt(jnp.sum(square, axis=0, keepdims=True) + 1e-06)
-    for i in range(STEPS):
-        part = pl.ds(i * step_rows, step_rows)
+
+    def normalize(i, carry):
+        part = pl.ds(pl.multiple_of(i * step_rows, step_rows), step_rows)
         unit[part, :] = (raw[part, :].astype(jnp.float32) * scale).astype(jnp.bfloat16)
-
-    own.wait()
+        return carry
+
+    lax.fori_loop(0, STEPS, normalize, 0)
+
     for j, c in enumerate(chip_peers):
         slot = c * 2 + core
         send_block(emb_ref, slot, e_send.at[j], partner).wait_recv()
@@ -147,7 +167,6 @@
         )
         copy.start()
         sent.append(copy)
-    width = raw.shape[1]
     knot = lax.broadcasted_iota(jnp.int32, (knots, width), 0).astype(jnp.float32) + 1.0
     pos = knot * SPACING
     target = jnp.exp(-0.5 * pos * pos)
@@ -208,7 +227,8 @@
         pairs[p].wait_recv()
         value = value + pair_in[p]
         for c in range(chips):
-            z_out[p, c] = value[c * per:(c + 1) * per]
+            z_own[p, c] = value[c * per:(c + 1) * per]
+            z_out[p, c] = to_wire(value[c * per:(c + 1) * per])
         for j, c in enumerate(chip_peers):
             copy = pltpu.make_async_remote_copy(
                 src_ref=z_out.at[p, c], dst_ref=z_in.at[p, chip], send_sem=z_send.at[p, j],
@@ -217,13 +237,13 @@
             copy.start()
             sent.append(copy)
     for p in range(PARTS):
-        value = z_out[p, chip]
+        value = z_own[p, chip]
         for j, c in enumerate(chip_peers):
             pltpu.make_async_remote_copy(
                 src_ref=z_out.at[p, c], dst_ref=z_in.at[p, c], send_sem=z_send.at[p, j],
                 recv_sem=z_recv.at[p, c], device_id=(b, c * 2 + core), device_id_type=MESH,
             ).wait_recv()
-            value = value + z_in[p, c]
+            value = value + from_wire(z_in[p, c])
         out_ref[:, p * columns:(p + 1) * columns] = value
     for copy in sent:
         copy.wait_send()
@@ -241,7 +261,7 @@
     return pl.pallas_call(
         functools.partial(kernel, nb, nd),
         out_shape=jax.ShapeDtypeStruct((per, depth), f32),
-        in_specs=[pl.BlockSpec(memory_space=pl.ANY)] * 2,
+        in_specs=[pl.BlockSpec(memory_space=pltpu.HBM)] * 2,
         out_specs=pl.BlockSpec(memory_space=pltpu.VMEM),
         scratch_shapes=[
             pltpu.VMEM((depth, width), bf16),
@@ -255,7 +275,8 @@
             pltpu.VMEM((PARTS, half, columns), f32),
             pltpu.VMEM((PARTS, half, columns), f32),
             pltpu.VMEM((PARTS, chips, per, columns), f32),
-            pltpu.VMEM((PARTS, chips, per, columns), f32),
+            pltpu.VMEM((PARTS, chips, per, columns), bf16),
+            pltpu.VMEM((PARTS, chips, per, columns), bf16),
             dma((STEPS,)),
             dma,
             dma((chips,)),
@@ -269,7 +290,7 @@
             dma((PARTS, chips)),
         ],
         compiler_params=pltpu.CompilerParams(
-            collective_id=0, has_side_effects=True, vmem_limit_bytes=48 * 1024 * 1024
+            collective_id=0, has_side_effects=True, vmem_limit_bytes=64 * 1024 * 1024
         ),
         name="sigreg_backward",
     )(embeddings, directions)

time: 25.8 us -> 23 us (0.89)
  Pallas kernels: 23 us -> 21.4 us
  local copies, waits for them, and re-layouts: 2.56 us -> 1.38 us
    pallas_call x1, Pallas kernels: 23 us -> 21.4 us  [local(): pl.pallas_call(functools.partial(kernel, nb, nd), out_shape=jax.ShapeDtyp...]
    unnamed x5 -> x1, local copies, waits for them, and re-layouts: 2.56 us -> 1.38 us
where the time goes in v2:
time: 23 us; the launch traced here: 22.8 us
  Pallas kernels  21.4 us (93%)
  local copies, waits for them, and re-layouts  1.38 us (6%)
    pallas_call x1, Pallas kernels, local(): pl.pallas_call(functools.partial(kernel, nb, nd), out_shape=jax.ShapeDtyp...  21.4 us
    unnamed x1, local copies, waits for them, and re-layouts  1.38 us

profile of v2, /device:TPU:0, one launch (start us, length us, event | category | flops | bytes accessed | tf_op | source)
XLA Modules:
  0.0 22.8 jit_solution(1479265782351915359)
XLA Ops:
  0.0 21.4 %sigreg_backward.1 = f32[4,2048]{1,0:T(4,128)} custom-call(bf16[4,2048]{1,0:T(4,128)(2,1)} %emb_ref.1, bf16[2048,256]{1,0:T(8,128)(2,1)} %dir_ref.1), custom_call_target="tpu_custom_call" | custom-call | tf_op jit(solution)/shard_map/sigreg_backward/pallas_call | solution.py:261
  21.4 1.4 %copy.4 = f32[4,2048]{1,0:T(4,128)} copy(f32[4,2048]{1,0:T(4,128)} %sigreg_backward.1) | data formatting | bytes 65536

commit v3 on v2

--- a/solution.py
+++ b/solution.py
@@ -12,6 +12,7 @@
 MESH = pl.DeviceIdType.MESH
 TILE = 16
 PARTS = 4
+GROUPS = 2
 STEPS = 8
 LIFT = 2.0 ** 50
 
@@ -43,7 +44,7 @@
 
 def kernel(
     nb, nd, emb_ref, dir_ref, out_ref,
-    raw, unit, blocks, rows_f32, waves, acc, sums, coef,
+    raw, unit, blocks, rows_f32, waves, acc, sums, coef, grads,
     pair_out, pair_in, z_own, z_out, z_in,
     raw_sem, own_sem, e_send, e_recv, f_send, s_send, s_recv, p_send, p_recv, z_send, z_recv,
 ):
@@ -119,17 +120,24 @@
         copy.start()
         sent.append(copy)
 
-    def project(which, side):
+    wide = width // GROUPS
+    knots = KNOTS - 1
+
+    def gather_rows(which, side):
         for c in range(chips):
             rows_f32[which, c * per:(c + 1) * per, :] = blocks[c * 2 + side].astype(jnp.float32)
+        return rows_f32[which].astype(jnp.bfloat16)
+
+    def project(rows, g):
         return jnp.dot(
-            rows_f32[which].astype(jnp.bfloat16), unit[...], preferred_element_type=jnp.float32
+            rows, unit[:, g * wide:(g + 1) * wide], preferred_element_type=jnp.float32
         )
 
     def fold(value):
         return jnp.sum(value.reshape(TILE // 8, 8, -1), axis=0)
 
-    def trig(which, projected):
+    def trig(which, projected, g):
+        lanes = pl.ds(g * wide, wide)
         for r in range(half // TILE):
             first = which == 0 and r == 0
             at = which * half + r * TILE
@@ -146,61 +154,67 @@
                         cosine * cosine1 - sine * sine1, sine * cosine1 + cosine * sine1
                     )
                 for s in range(2):
-                    waves[k - 1, s, at:at + TILE, :] = powers[k][s]
+                    waves[k - 1, s, at:at + TILE, lanes] = powers[k][s]
                     part = fold(powers[k][s])
-                    acc[s, k - 1] = part if first else acc[s, k - 1] + part
-
-    trig(0, project(0, core))
+                    rows = pl.ds((s * knots + k - 1) * 8, 8)
+                    acc[g, rows, :] = part if first else acc[g, rows, :] + part
+
+    home_rows = gather_rows(0, core)
+    for g in range(GROUPS):
+        trig(0, project(home_rows, g), g)
     send_rest = [lax.rem(chip + j, chips) * 2 + other for j in range(chips)]
     for slot in send_rest:
         send_block(emb_ref, slot, e_send.at[0], partner).wait_recv()
-    trig(1, project(1, other))
-
-    knots = KNOTS - 1
-    for s in range(2):
-        sums[b, s * knots:(s + 1) * knots, :] = jnp.sum(acc[s], axis=1)
-    mine = sums.at[b]
-    for j, a in enumerate(batch_peers):
-        copy = pltpu.make_async_remote_copy(
-            src_ref=mine, dst_ref=sums.at[b], send_sem=s_send.at[j], recv_sem=s_recv.at[b],
-            device_id=(a, d), device_id_type=MESH,
-        )
-        copy.start()
-        sent.append(copy)
-    knot = lax.broadcasted_iota(jnp.int32, (knots, width), 0).astype(jnp.float32) + 1.0
+    away_rows = gather_rows(1, other)
+
+    def send_sums(g, j, a, slot):
+        return pltpu.make_async_remote_copy(
+            src_ref=sums.at[g, b], dst_ref=sums.at[g, slot], send_sem=s_send.at[g, j],
+            recv_sem=s_recv.at[g, slot], device_id=(a, d), device_id_type=MESH,
+        )
+
+    for g in range(GROUPS):
+        trig(1, project(away_rows, g), g)
+        value = acc[g, pl.ds(0, 2 * knots, stride=8), :]
+        for i in range(1, 8):
+            value = value + acc[g, pl.ds(i, 2 * knots, stride=8), :]
+        sums[g, b] = value
+        for j, a in enumerate(batch_peers):
+            copy = send_sums(g, j, a, b)
+            copy.start()
+            sent.append(copy)
+    knot = lax.broadcasted_iota(jnp.int32, (knots, wide), 0).astype(jnp.float32) + 1.0
     pos = knot * SPACING
     target = jnp.exp(-0.5 * pos * pos)
     ends = jnp.where(knot == float(knots), 0.5, 1.0)
     weight = 2.0 * (ends * SPACING * target)
-    for j, a in enumerate(batch_peers):
-        pltpu.make_async_remote_copy(
-            src_ref=mine, dst_ref=sums.at[a], send_sem=s_send.at[j], recv_sem=s_recv.at[a],
-            device_id=(a, d), device_id_type=MESH,
-        ).wait_recv()
-    total = sums[0]
-    for a in range(1, nb):
-        total = total + sums[a]
-    mean = total * (1.0 / total_rows)
-    coef[0:knots, :] = pos * (weight * (mean[0:knots] - target))
-    coef[knots:2 * knots, :] = pos * (weight * mean[knots:2 * knots])
-    ones = jnp.full((1, width), 1.0, jnp.float32)
-    zeros = jnp.zeros((1, width), jnp.float32)
+
+    def coefficients(g):
+        for j, a in enumerate(batch_peers):
+            send_sums(g, j, a, a).wait_recv()
+        total = sums[g, 0]
+        for a in range(1, nb):
+            total = total + sums[g, a]
+        mean = total * (1.0 / total_rows)
+        coef[g, 0:knots, :] = pos * (weight * (mean[0:knots] - target))
+        coef[g, knots:2 * knots, :] = pos * (weight * mean[knots:2 * knots])
+
+    ones = jnp.full((1, wide), 1.0, jnp.float32)
+    zeros = jnp.zeros((1, wide), jnp.float32)
     end = 2.0 * 0.5 * SPACING
     first_term = 0.0 * (ones * (end * zeros) - zeros * (end * (ones - 1.0)))
 
-    def grad(which):
-        tiles = []
+    def grad(which, g):
+        lanes = pl.ds(g * wide, wide)
         for r in range(half // TILE):
             at = which * half + r * TILE
-            value = jnp.broadcast_to(first_term, (TILE, width))
+            value = jnp.broadcast_to(first_term, (TILE, wide))
             for k in range(knots):
                 value = value + (
-                    waves[k, 0, at:at + TILE, :] * coef[knots + k:knots + k + 1, :]
-                    - waves[k, 1, at:at + TILE, :] * coef[k:k + 1, :]
+                    waves[k, 0, at:at + TILE, lanes] * coef[g, knots + k:knots + k + 1, :]
+                    - waves[k, 1, at:at + TILE, lanes] * coef[g, k:k + 1, :]
                 )
-            tiles.append(value)
-        value = tiles[0] if len(tiles) == 1 else jnp.concatenate(tiles, axis=0)
-        return value.astype(jnp.bfloat16)
+            grads[at:at + TILE, lanes] = value.astype(jnp.bfloat16)
 
     columns = depth // PARTS
 
@@ -210,7 +224,12 @@
             preferred_element_type=jnp.float32,
         )
 
-    away = grad(1)
+    for g in range(GROUPS):
+        coefficients(g)
+        grad(1, g)
+        if g + 1 < GROUPS:
+            grad(0, g)
+    away = grads[half:2 * half, :]
     pairs = []
     for p in range(PARTS):
         pair_out[p] = back(away, p)
@@ -221,7 +240,8 @@
         copy.start()
         pairs.append(copy)
         sent.append(copy)
-    home = grad(0)
+    grad(0, GROUPS - 1)
+    home = grads[0:half, :]
     for p in range(PARTS):
         value = back(home, p)
         pairs[p].wait_recv()
@@ -256,6 +276,7 @@
     half = chips * per
     knots = KNOTS - 1
     columns = depth // PARTS
+    wide = width // GROUPS
     f32, bf16 = jnp.float32, jnp.bfloat16
     dma = pltpu.SemaphoreType.DMA
     return pl.pallas_call(
@@ -269,9 +290,10 @@
             pltpu.VMEM((nd, per, depth), bf16),
             pltpu.VMEM((2, half, depth), f32),
             pltpu.VMEM((knots, 2, 2 * half, width), f32),
-            pltpu.VMEM((2, knots, 8, width), f32),
-            pltpu.VMEM((nb, 2 * knots, width), f32),
-            pltpu.VMEM((2 * knots, width), f32),
+            pltpu.VMEM((GROUPS, 2 * knots * 8, wide), f32),
+            pltpu.VMEM((GROUPS, nb, 2 * knots, wide), f32),
+            pltpu.VMEM((GROUPS, 2 * knots, wide), f32),
+            pltpu.VMEM((2 * half, width), bf16),
             pltpu.VMEM((PARTS, half, columns), f32),
             pltpu.VMEM((PARTS, half, columns), f32),
             pltpu.VMEM((PARTS, chips, per, columns), f32),
@@ -282,8 +304,8 @@
             dma((chips,)),
             dma((nd,)),
             dma((chips,)),
-            dma((nb,)),
-            dma((nb,)),
+            dma((GROUPS, nb)),
+            dma((GROUPS, nb)),
             dma((PARTS,)),
             dma((PARTS,)),
             dma((PARTS, chips)),

time: 23 us -> 22.8 us (level)
  no operation moved by 1% of the time
where the time goes in v3:
time: 22.8 us; the launch traced here: 22.7 us
  Pallas kernels  21.3 us (93%)
  local copies, waits for them, and re-layouts  1.38 us (6%)
    pallas_call x1, Pallas kernels, local(): pl.pallas_call(functools.partial(kernel, nb, nd), out_shape=jax.ShapeDtyp...  21.3 us
    unnamed x1, local copies, waits for them, and re-layouts  1.38 us

profile of v3, /device:TPU:0, one launch (start us, length us, event | category | flops | bytes accessed | tf_op | source)
XLA Modules:
  0.0 22.7 jit_solution(505357660153156687)
XLA Ops:
  0.0 21.3 %sigreg_backward.1 = f32[4,2048]{1,0:T(4,128)} custom-call(bf16[4,2048]{1,0:T(4,128)(2,1)} %emb_ref.1, bf16[2048,256]{1,0:T(8,128)(2,1)} %dir_ref.1), custom_call_target="tpu_custom_call" | custom-call | tf_op jit(solution)/shard_map/sigreg_backward/pallas_call | solution.py:282
  21.3 1.4 %copy.4 = f32[4,2048]{1,0:T(4,128)} copy(f32[4,2048]{1,0:T(4,128)} %sigreg_backward.1) | data formatting | bytes 65536

commit v4 on v3

--- a/solution.py
+++ b/solution.py
@@ -45,7 +45,7 @@
 def kernel(
     nb, nd, emb_ref, dir_ref, out_ref,
     raw, unit, blocks, rows_f32, waves, acc, sums, coef, grads,
-    pair_out, pair_in, z_own, z_out, z_in,
+    kept, pair_out, pair_in, z_own, z_out, z_in,
     raw_sem, own_sem, e_send, e_recv, f_send, s_send, s_recv, p_send, p_recv, z_send, z_recv,
 ):
     chips = nd // 2
@@ -226,13 +226,14 @@
 
     for g in range(GROUPS):
         coefficients(g)
-        grad(1, g)
-        if g + 1 < GROUPS:
-            grad(0, g)
-    away = grads[half:2 * half, :]
+        for which in range(2):
+            grad(which, g)
+    both = grads[...]
     pairs = []
     for p in range(PARTS):
-        pair_out[p] = back(away, p)
+        value = back(both, p)
+        kept[p] = value[0:half]
+        pair_out[p] = value[half:2 * half]
         copy = pltpu.make_async_remote_copy(
             src_ref=pair_out.at[p], dst_ref=pair_in.at[p], send_sem=p_send.at[p],
             recv_sem=p_recv.at[p], device_id=partner, device_id_type=MESH,
@@ -240,12 +241,9 @@
         copy.start()
         pairs.append(copy)
         sent.append(copy)
-    grad(0, GROUPS - 1)
-    home = grads[0:half, :]
     for p in range(PARTS):
-        value = back(home, p)
         pairs[p].wait_recv()
-        value = value + pair_in[p]
+        value = kept[p] + pair_in[p]
         for c in range(chips):
             z_own[p, c] = value[c * per:(c + 1) * per]
             z_out[p, c] = to_wire(value[c * per:(c + 1) * per])
@@ -296,6 +294,7 @@
             pltpu.VMEM((2 * half, width), bf16),
             pltpu.VMEM((PARTS, half, columns), f32),
             pltpu.VMEM((PARTS, half, columns), f32),
+            pltpu.VMEM((PARTS, half, columns), f32),
             pltpu.VMEM((PARTS, chips, per, columns), f32),
             pltpu.VMEM((PARTS, chips, per, columns), bf16),
             pltpu.VMEM((PARTS, chips, per, columns), bf16),
@@ -312,7 +311,7 @@
             dma((PARTS, chips)),
         ],
         compiler_params=pltpu.CompilerParams(
-            collective_id=0, has_side_effects=True, vmem_limit_bytes=64 * 1024 * 1024
+            collective_id=0, has_side_effects=True, vmem_limit_bytes=56 * 1000 * 1000
         ),
         name="sigreg_backward",
     )(embeddings, directions)

time: 22.8 us -> 22.1 us (0.969)
  Pallas kernels: 21.3 us -> 20.5 us
    pallas_call x1, Pallas kernels: 21.3 us -> 20.5 us  [local(): pl.pallas_call(functools.partial(kernel, nb, nd), out_shape=jax.ShapeDtyp...]
    unnamed x1 -> x3, local copies, waits for them, and re-layouts: 1.38 us -> 1.33 us
where the time goes in v4:
time: 22.1 us; the launch traced here: 21.9 us
  Pallas kernels  20.5 us (93%)
  local copies, waits for them, and re-layouts  1.33 us (6%)
    pallas_call x1, Pallas kernels, local(): pl.pallas_call(functools.partial(kernel, nb, nd), out_shape=jax.ShapeDtyp...  20.5 us
    unnamed x3, local copies, waits for them, and re-layouts  1.33 us

profile of v4, /device:TPU:0, one launch (start us, length us, event | category | flops | bytes accessed | tf_op | source)
XLA Modules:
  0.0 21.9 jit_solution(8292310496678069986)
XLA Ops:
  0.0 0.0 copy-start
  0.0 0.7 %copy-done = bf16[4,2048]{1,0:T(4,128)(2,1)S(1)} copy-done((bf16[4,2048]{1,0:T(4,128)(2,1)S(1)}, bf16[4,2048]{1,0:T(4,128)(2,1)}, u32[]{:S(2)}) %copy-start) | copy-done | bytes 16408
  0.7 20.5 %sigreg_backward.1 = f32[4,2048]{1,0:T(4,128)S(1)} custom-call(bf16[4,2048]{1,0:T(4,128)(2,1)S(1)} %copy-done, bf16[2048,256]{1,0:T(8,128)(2,1)} %dir_ref.1), custom_call_target="tpu_custom_call" | custom-call | tf_op jit(solution)/shard_map/sigreg_backward/pallas_call | solution.py:280
  21.2 0.6 %copy.4 = f32[4,2048]{1,0:T(4,128)} copy(f32[4,2048]{1,0:T(4,128)S(1)} %sigreg_backward.1) | data formatting | bytes 65536
Async XLA Ops:
  0.0 0.7 %copy-start = (bf16[4,2048]{1,0:T(4,128)(2,1)S(1)}, bf16[4,2048]{1,0:T(4,128)(2,1)}, u32[]{:S(2)}) copy-start(bf16[4,2048]{1,0:T(4,128)(2,1)} %emb_ref.1) | copy-start | bytes 49156

commit v5 on v4

--- a/solution.py
+++ b/solution.py
@@ -72,11 +72,12 @@
     batch_peers = [lax.rem(b + j, nb) for j in range(1, nb)]
     barrier = pltpu.get_barrier_semaphore()
     for c in chip_peers:
-        pl.semaphore_signal(barrier, inc=1, device_id=(b, c * 2 + core), device_id_type=MESH)
+        for side in (core, other):
+            pl.semaphore_signal(barrier, inc=1, device_id=(b, c * 2 + side), device_id_type=MESH)
     for a in batch_peers:
         pl.semaphore_signal(barrier, inc=1, device_id=(a, d), device_id_type=MESH)
     pl.semaphore_signal(barrier, inc=1, device_id=partner, device_id_type=MESH)
-    pl.semaphore_wait(barrier, len(chip_peers) + len(batch_peers) + 1)
+    pl.semaphore_wait(barrier, 2 * len(chip_peers) + len(batch_peers) + 1)
 
     def send_block(src, slot, sem, device):
         return pltpu.make_async_remote_copy(
@@ -93,6 +94,10 @@
     copy = send_block(blocks.at[d], d, e_send.at[chips - 1], partner)
     copy.start()
     sent.append(copy)
+    for j, c in enumerate(chip_peers):
+        copy = send_block(blocks.at[d], d, f_send.at[j], (b, c * 2 + other))
+        copy.start()
+        sent.append(copy)
 
     for load in loads:
         load.wait()
@@ -116,9 +121,6 @@
     for j, c in enumerate(chip_peers):
         slot = c * 2 + core
         send_block(emb_ref, slot, e_send.at[j], partner).wait_recv()
-        copy = send_block(blocks.at[slot], slot, f_send.at[j], partner)
-        copy.start()
-        sent.append(copy)
 
     wide = width // GROUPS
     knots = KNOTS - 1

time: 22.1 us -> 22.2 us (level)
  no operation moved by 1% of the time
where the time goes in v5:
time: 22.2 us; the launch traced here: 21.9 us
  Pallas kernels  20.6 us (93%)
  local copies, waits for them, and re-layouts  1.33 us (6%)
    pallas_call x1, Pallas kernels, local(): pl.pallas_call(functools.partial(kernel, nb, nd), out_shape=jax.ShapeDtyp...  20.6 us
    unnamed x3, local copies, waits for them, and re-layouts  1.33 us

profile of v5, /device:TPU:0, one launch (start us, length us, event | category | flops | bytes accessed | tf_op | source)
XLA Modules:
  0.0 21.9 jit_solution(3223227610326453123)
XLA Ops:
  0.0 0.0 copy-start
  0.0 0.7 %copy-done = bf16[4,2048]{1,0:T(4,128)(2,1)S(1)} copy-done((bf16[4,2048]{1,0:T(4,128)(2,1)S(1)}, bf16[4,2048]{1,0:T(4,128)(2,1)}, u32[]{:S(2)}) %copy-start) | copy-done | bytes 16408
  0.7 20.6 %sigreg_backward.1 = f32[4,2048]{1,0:T(4,128)S(1)} custom-call(bf16[4,2048]{1,0:T(4,128)(2,1)S(1)} %copy-done, bf16[2048,256]{1,0:T(8,128)(2,1)} %dir_ref.1), custom_call_target="tpu_custom_call" | custom-call | tf_op jit(solution)/shard_map/sigreg_backward/pallas_call | solution.py:282
  21.3 0.6 %copy.4 = f32[4,2048]{1,0:T(4,128)} copy(f32[4,2048]{1,0:T(4,128)S(1)} %sigreg_backward.1) | data formatting | bytes 65536
Async XLA Ops:
  0.0 0.7 %copy-start = (bf16[4,2048]{1,0:T(4,128)(2,1)S(1)}, bf16[4,2048]{1,0:T(4,128)(2,1)}, u32[]{:S(2)}) copy-start(bf16[4,2048]{1,0:T(4,128)(2,1)} %emb_ref.1) | copy-start | bytes 49156

commit v6 on v5

--- a/solution.py
+++ b/solution.py
@@ -11,7 +11,6 @@
 SPACING = 3.0 / (KNOTS - 1)
 MESH = pl.DeviceIdType.MESH
 TILE = 16
-PARTS = 4
 GROUPS = 2
 STEPS = 8
 LIFT = 2.0 ** 50
@@ -46,7 +45,7 @@
     nb, nd, emb_ref, dir_ref, out_ref,
     raw, unit, blocks, rows_f32, waves, acc, sums, coef, grads,
     kept, pair_out, pair_in, z_own, z_out, z_in,
-    raw_sem, own_sem, e_send, e_recv, f_send, s_send, s_recv, p_send, p_recv, z_send, z_recv,
+    raw_sem, own_sem, e_send, e_recv, s_send, s_recv, p_send, p_recv, z_send, z_recv,
 ):
     chips = nd // 2
     half = chips * emb_ref.shape[0]
@@ -65,8 +64,14 @@
         load = pltpu.make_async_copy(dir_ref.at[part], raw.at[part], raw_sem.at[i])
         load.start()
         loads.append(load)
-    own = pltpu.make_async_copy(emb_ref, blocks.at[d], own_sem)
-    own.start()
+    mid = depth // 2
+    own = []
+    for h in range(2):
+        copy = pltpu.make_async_copy(
+            emb_ref.at[:, pl.ds(h * mid, mid)], blocks.at[h, d], own_sem.at[h]
+        )
+        copy.start()
+        own.append(copy)
 
     chip_peers = [lax.rem(chip + j, chips) for j in range(1, chips)]
     batch_peers = [lax.rem(b + j, nb) for j in range(1, nb)]
@@ -79,25 +84,33 @@
     pl.semaphore_signal(barrier, inc=1, device_id=partner, device_id_type=MESH)
     pl.semaphore_wait(barrier, 2 * len(chip_peers) + len(batch_peers) + 1)
 
-    def send_block(src, slot, sem, device):
-        return pltpu.make_async_remote_copy(
-            src_ref=src, dst_ref=blocks.at[slot], send_sem=sem, recv_sem=e_recv.at[slot],
+    sent = []
+
+    def send_block(h, slot, device):
+        copy = pltpu.make_async_remote_copy(
+            src_ref=blocks.at[h, slot], dst_ref=blocks.at[h, slot],
+            send_sem=e_send.at[len(sent)], recv_sem=e_recv.at[h, slot],
             device_id=device, device_id_type=MESH,
         )
-
-    sent = []
-    own.wait()
-    for j, c in enumerate(chip_peers):
-        copy = send_block(blocks.at[d], d, e_send.at[j], (b, c * 2 + core))
         copy.start()
         sent.append(copy)
-    copy = send_block(blocks.at[d], d, e_send.at[chips - 1], partner)
-    copy.start()
-    sent.append(copy)
-    for j, c in enumerate(chip_peers):
-        copy = send_block(blocks.at[d], d, f_send.at[j], (b, c * 2 + other))
-        copy.start()
-        sent.append(copy)
+
+    def take_block(h, slot):
+        pltpu.make_async_remote_copy(
+            src_ref=blocks.at[h, slot], dst_ref=blocks.at[h, slot],
+            send_sem=e_send.at[0], recv_sem=e_recv.at[h, slot],
+            device_id=partner, device_id_type=MESH,
+        ).wait_recv()
+
+    for copy in own:
+        copy.wait()
+    for h in range(2):
+        for c in chip_peers:
+            send_block(h, d, (b, c * 2 + core))
+    for h in range(2):
+        send_block(h, d, partner)
+    for c in chip_peers:
+        send_block(1, d, (b, c * 2 + other))
 
     for load in loads:
         load.wait()
@@ -118,16 +131,21 @@
 
     lax.fori_loop(0, STEPS, normalize, 0)
 
-    for j, c in enumerate(chip_peers):
-        slot = c * 2 + core
-        send_block(emb_ref, slot, e_send.at[j], partner).wait_recv()
+    for c in chip_peers:
+        take_block(0, c * 2 + core)
+        send_block(0, c * 2 + core, partner)
+    for c in chip_peers:
+        take_block(1, c * 2 + core)
 
     wide = width // GROUPS
     knots = KNOTS - 1
 
     def gather_rows(which, side):
         for c in range(chips):
-            rows_f32[which, c * per:(c + 1) * per, :] = blocks[c * 2 + side].astype(jnp.float32)
+            for h in range(2):
+                rows_f32[which, c * per:(c + 1) * per, h * mid:(h + 1) * mid] = blocks[
+                    h, c * 2 + side
+                ].astype(jnp.float32)
         return rows_f32[which].astype(jnp.bfloat16)
 
     def project(rows, g):
@@ -164,9 +182,9 @@
     home_rows = gather_rows(0, core)
     for g in range(GROUPS):
         trig(0, project(home_rows, g), g)
-    send_rest = [lax.rem(chip + j, chips) * 2 + other for j in range(chips)]
-    for slot in send_rest:
-        send_block(emb_ref, slot, e_send.at[0], partner).wait_recv()
+    for h in range(2):
+        for j in range(chips):
+            take_block(h, lax.rem(chip + j, chips) * 2 + other)
     away_rows = gather_rows(1, other)
 
     def send_sums(g, j, a, slot):
@@ -218,53 +236,72 @@
                 )
             grads[at:at + TILE, lanes] = value.astype(jnp.bfloat16)
 
-    columns = depth // PARTS
-
-    def back(value, p):
-        return lax.dot_general(
-            value, unit[p * columns:(p + 1) * columns, :], (((1,), (1,)), ((), ())),
-            preferred_element_type=jnp.float32,
-        )
-
     for g in range(GROUPS):
         coefficients(g)
         for which in range(2):
             grad(which, g)
     both = grads[...]
-    pairs = []
-    for p in range(PARTS):
-        value = back(both, p)
-        kept[p] = value[0:half]
-        pair_out[p] = value[half:2 * half]
-        copy = pltpu.make_async_remote_copy(
-            src_ref=pair_out.at[p], dst_ref=pair_in.at[p], send_sem=p_send.at[p],
-            recv_sem=p_recv.at[p], device_id=partner, device_id_type=MESH,
-        )
-        copy.start()
-        pairs.append(copy)
-        sent.append(copy)
-    for p in range(PARTS):
-        pairs[p].wait_recv()
-        value = kept[p] + pair_in[p]
+
+    def back(p):
+        return lax.dot_general(
+            both, unit[p * mid:(p + 1) * mid, :], (((1,), (1,)), ((), ())),
+            preferred_element_type=jnp.float32,
+        )
+
+    def send_sum(p, i, src, slot, device):
+        return pltpu.make_async_remote_copy(
+            src_ref=src, dst_ref=z_in.at[p, slot], send_sem=z_send.at[p, i],
+            recv_sem=z_recv.at[p, slot], device_id=device, device_id_type=MESH,
+        )
+
+    value = back(1)
+    kept[...] = value[0:half]
+    pair_out[...] = value[half:2 * half]
+    pair = pltpu.make_async_remote_copy(
+        src_ref=pair_out, dst_ref=pair_in, send_sem=p_send, recv_sem=p_recv,
+        device_id=partner, device_id_type=MESH,
+    )
+    pair.start()
+    sent.append(pair)
+    value = back(0)
+    for side in range(2):
         for c in range(chips):
-            z_own[p, c] = value[c * per:(c + 1) * per]
-            z_out[p, c] = to_wire(value[c * per:(c + 1) * per])
-        for j, c in enumerate(chip_peers):
-            copy = pltpu.make_async_remote_copy(
-                src_ref=z_out.at[p, c], dst_ref=z_in.at[p, chip], send_sem=z_send.at[p, j],
-                recv_sem=z_recv.at[p, chip], device_id=(b, c * 2 + core), device_id_type=MESH,
-            )
+            rows = value[side * half + c * per:side * half + (c + 1) * per]
+            if side == 0:
+                z_own[0, c] = rows
+            z_out[0, side, c] = to_wire(rows)
+    for i, c in enumerate(chip_peers):
+        for side, target in ((0, core), (1, other)):
+            copy = send_sum(0, side * chips + i, z_out.at[0, side, c], d, (b, c * 2 + target))
             copy.start()
             sent.append(copy)
-    for p in range(PARTS):
-        value = z_own[p, chip]
-        for j, c in enumerate(chip_peers):
-            pltpu.make_async_remote_copy(
-                src_ref=z_out.at[p, c], dst_ref=z_in.at[p, c], send_sem=z_send.at[p, j],
-                recv_sem=z_recv.at[p, c], device_id=(b, c * 2 + core), device_id_type=MESH,
-            ).wait_recv()
-            value = value + from_wire(z_in[p, c])
-        out_ref[:, p * columns:(p + 1) * columns] = value
+    copy = send_sum(0, chips - 1, z_out.at[0, 1, chip], d, partner)
+    copy.start()
+    sent.append(copy)
+    pair.wait_recv()
+    value = kept[...] + pair_in[...]
+    for c in range(chips):
+        rows = value[c * per:(c + 1) * per]
+        z_own[1, c] = rows
+        z_out[1, 0, c] = to_wire(rows)
+    for i, c in enumerate(chip_peers):
+        copy = send_sum(1, i, z_out.at[1, 0, c], d, (b, c * 2 + core))
+        copy.start()
+        sent.append(copy)
+
+    def take_sum(p, slot):
+        send_sum(p, 0, z_out.at[0, 0, 0], slot, partner).wait_recv()
+        return from_wire(z_in[p, slot])
+
+    value = z_own[0, chip] + take_sum(0, chip * 2 + other)
+    for c in chip_peers:
+        for side in (core, other):
+            value = value + take_sum(0, c * 2 + side)
+    out_ref[:, 0:mid] = value
+    value = z_own[1, chip]
+    for c in chip_peers:
+        value = value + take_sum(1, c * 2 + core)
+    out_ref[:, mid:depth] = value
     for copy in sent:
         copy.wait_send()
 
@@ -275,7 +312,7 @@
     chips = nd // 2
     half = chips * per
     knots = KNOTS - 1
-    columns = depth // PARTS
+    mid = depth // 2
     wide = width // GROUPS
     f32, bf16 = jnp.float32, jnp.bfloat16
     dma = pltpu.SemaphoreType.DMA
@@ -287,30 +324,29 @@
         scratch_shapes=[
             pltpu.VMEM((depth, width), bf16),
             pltpu.VMEM((depth, width), bf16),
-            pltpu.VMEM((nd, per, depth), bf16),
+            pltpu.VMEM((2, nd, per, mid), bf16),
             pltpu.VMEM((2, half, depth), f32),
             pltpu.VMEM((knots, 2, 2 * half, width), f32),
             pltpu.VMEM((GROUPS, 2 * knots * 8, wide), f32),
             pltpu.VMEM((GROUPS, nb, 2 * knots, wide), f32),
             pltpu.VMEM((GROUPS, 2 * knots, wide), f32),
             pltpu.VMEM((2 * half, width), bf16),
-            pltpu.VMEM((PARTS, half, columns), f32),
-            pltpu.VMEM((PARTS, half, columns), f32),
-            pltpu.VMEM((PARTS, half, columns), f32),
-            pltpu.VMEM((PARTS, chips, per, columns), f32),
-            pltpu.VMEM((PARTS, chips, per, columns), bf16),
-            pltpu.VMEM((PARTS, chips, per, columns), bf16),
+            pltpu.VMEM((half, mid), f32),
+            pltpu.VMEM((half, mid), f32),
+            pltpu.VMEM((half, mid), f32),
+            pltpu.VMEM((2, chips, per, mid), f32),
+            pltpu.VMEM((2, 2, chips, per, mid), bf16),
+            pltpu.VMEM((2, nd, per, mid), bf16),
             dma((STEPS,)),
-            dma,
-            dma((chips,)),
-            dma((nd,)),
-            dma((chips,)),
+            dma((2,)),
+            dma((4 * chips,)),
+            dma((2, nd)),
             dma((GROUPS, nb)),
             dma((GROUPS, nb)),
-            dma((PARTS,)),
-            dma((PARTS,)),
-            dma((PARTS, chips)),
-            dma((PARTS, chips)),
+            dma,
+            dma,
+            dma((2, nd)),
+            dma((2, nd)),
         ],
         compiler_params=pltpu.CompilerParams(
             collective_id=0, has_side_effects=True, vmem_limit_bytes=56 * 1000 * 1000

time: 22.2 us -> 22.3 us (level)
  no operation moved by 1% of the time
where the time goes in v6:
time: 22.3 us; the launch traced here: 22 us
  Pallas kernels  20.7 us (93%)
  local copies, waits for them, and re-layouts  1.33 us (6%)
    pallas_call x1, Pallas kernels, local(): pl.pallas_call(functools.partial(kernel, nb, nd), out_shape=jax.ShapeDtyp...  20.7 us
    unnamed x3, local copies, waits for them, and re-layouts  1.33 us

profile of v6, /device:TPU:0, one launch (start us, length us, event | category | flops | bytes accessed | tf_op | source)
XLA Modules:
  0.0 22.0 jit_solution(14658142376968678177)
XLA Ops:
  0.0 0.0 copy-start
  0.0 0.7 %copy-done = bf16[4,2048]{1,0:T(4,128)(2,1)S(1)} copy-done((bf16[4,2048]{1,0:T(4,128)(2,1)S(1)}, bf16[4,2048]{1,0:T(4,128)(2,1)}, u32[]{:S(2)}) %copy-start) | copy-done | bytes 16408
  0.7 20.7 %sigreg_backward.1 = f32[4,2048]{1,0:T(4,128)S(1)} custom-call(bf16[4,2048]{1,0:T(4,128)(2,1)S(1)} %copy-done, bf16[2048,256]{1,0:T(8,128)(2,1)} %dir_ref.1), custom_call_target="tpu_custom_call" | custom-call | tf_op jit(solution)/shard_map/sigreg_backward/pallas_call | solution.py:319
  21.4 0.6 %copy.4 = f32[4,2048]{1,0:T(4,128)} copy(f32[4,2048]{1,0:T(4,128)S(1)} %sigreg_backward.1) | data formatting | bytes 65536
Async XLA Ops:
  0.0 0.7 %copy-start = (bf16[4,2048]{1,0:T(4,128)(2,1)S(1)}, bf16[4,2048]{1,0:T(4,128)(2,1)}, u32[]{:S(2)}) copy-start(bf16[4,2048]{1,0:T(4,128)(2,1)} %emb_ref.1) | copy-start | bytes 49156

commit v7 on v2

v7 whole, which is shorter than its diff:
```python
import functools

import jax
import jax.numpy as jnp
from jax import lax
from jax.experimental import pallas as pl
from jax.experimental.pallas import tpu as pltpu
from jax.sharding import PartitionSpec as P

KNOTS = 17
SPACING = 3.0 / (KNOTS - 1)
MESH = pl.DeviceIdType.MESH
TILE = 16
PARTS = 2
STEPS = 8
LIFT = 2.0 ** 50


def to_wire(value):
    value = value * LIFT
    return (value * jnp.abs(value)).astype(jnp.bfloat16)


def from_wire(value):
    value = value.astype(jnp.float32)
    return value * lax.rsqrt(jnp.maximum(jnp.abs(value), 2.0 ** -126)) * (1.0 / LIFT)


def sin_cos(angle):
    n = jnp.round(angle * 0.15915494309189535)
    rest = ((angle - n * 6.28125) - n * 1.9350051879882812e-3) - n * 3.019915981956753e-7
    rest = rest * 0.25
    z = rest * rest
    sine = rest + rest * z * (-1.6666654611e-1 + z * (8.3321608736e-3 - z * 1.9515295891e-4))
    cosine = 1.0 - 0.5 * z + z * z * (
        4.166664568298827e-2 + z * (-1.388731625493765e-3 + z * 2.443315711809948e-5)
    )
    for _ in range(2):
        twice = sine + sine
        sine, cosine = twice * cosine, 1.0 - twice * sine
    return sine, cosine


def kernel(
    nb, nd, emb_ref, dir_ref, out_ref,
    raw, unit, blocks, rows_f32, waves, acc, sums, coef, grads,
    kept, pair_out, pair_in, z_own, z_out, z_in,
    raw_sem, own_sem, e_send, e_recv, f_send, f_recv, s_send, s_recv, p_send, p_recv, z_send, z_recv,
):
    chips = nd // 2
    half = chips * emb_ref.shape[0]
    per = emb_ref.shape[0]
    depth = raw.shape[0]
    total_rows = half * 2 * nb
    b, d = lax.axis_index("batch"), lax.axis_index("dir")
    chip, core = d // 2, lax.rem(d, 2)
    other = 1 - core
    partner = (b, chip * 2 + other)
    step_rows = depth // STEPS

    def remote(src, dst, send_sem, recv_sem, device):
        return pltpu.make_async_remote_copy(
            src_ref=src, dst_ref=dst, send_sem=send_sem, recv_sem=recv_sem,
            device_id=device, device_id_type=MESH,
        )

    def wait_all(ref, sem):
        pltpu.make_async_copy(ref, ref, sem).wait()

    load = pltpu.make_async_copy(dir_ref, raw, raw_sem)
    load.start()
    own = pltpu.make_async_copy(emb_ref, blocks.at[core, chip], own_sem)
    own.start()

    chip_peers = [lax.rem(chip + j, chips) for j in range(1, chips)]
    batch_peers = [lax.rem(b + j, nb) for j in range(1, nb)]
    barrier = pltpu.get_barrier_semaphore()
    for c in chip_peers:
        pl.semaphore_signal(barrier, inc=1, device_id=(b, c * 2 + core), device_id_type=MESH)
    for a in batch_peers:
        pl.semaphore_signal(barrier, inc=1, device_id=(a, d), device_id_type=MESH)
    pl.semaphore_signal(barrier, inc=1, device_id=partner, device_id_type=MESH)
    pl.semaphore_wait(barrier, len(chip_peers) + len(batch_peers) + 1)

    mine = blocks.at[core, chip]
    own.wait()
    for c in chip_peers:
        remote(mine, mine, e_send, e_recv.at[chip], (b, c * 2 + core)).start()
    remote(mine, mine, e_send, f_recv, partner).start()

    load.wait()
    width = raw.shape[1]

    def add_squares(i, square):
        part = pl.ds(pl.multiple_of(i * step_rows, step_rows), step_rows)
        value = raw[part, :].astype(jnp.float32)
        return square + jnp.sum((value * value).reshape(step_rows // 8, 8, width), axis=0)

    square = lax.fori_loop(0, STEPS, add_squares, jnp.zeros((8, width), jnp.float32))
    scale = 1.0 / jnp.sqrt(jnp.sum(square, axis=0, keepdims=True) + 1e-06)

    def normalize(i, carry):
        part = pl.ds(pl.multiple_of(i * step_rows, step_rows), step_rows)
        unit[part, :] = (raw[part, :].astype(jnp.float32) * scale).astype(jnp.bfloat16)
        return carry

    lax.fori_loop(0, STEPS, normalize, 0)

    for c in chip_peers:
        block = blocks.at[core, c]
        remote(block, block, f_send, e_recv.at[c], partner).wait_recv()
        remote(block, block, f_send, f_recv, partner).start()

    knots = KNOTS - 1

    def project(which, side):
        for c in range(chips):
            rows_f32[c * per:(c + 1) * per, :] = blocks[side, c].astype(jnp.float32)
        return jnp.dot(
            rows_f32[...].astype(jnp.bfloat16), unit[...], preferred_element_type=jnp.float32
        )

    def fold(value):
        return jnp.sum(value.reshape(TILE // 8, 8, -1), axis=0)

    def trig(which, projected):
        for r in range(half // TILE):
            first = which == 0 and r == 0
            at = which * half + r * TILE
            sine1, cosine1 = sin_cos(SPACING * projected[r * TILE:(r + 1) * TILE])
            powers = {1: (cosine1, sine1)}
            for k in range(1, KNOTS):
                if k > 1 and k % 2 == 0:
                    cosine, sine = powers[k // 2]
                    twice = cosine + cosine
                    powers[k] = (twice * cosine - 1.0, twice * sine)
                elif k > 1:
                    (cos_a, sin_a), (cos_b, sin_b) = powers[k // 2], powers[k // 2 + 1]
                    powers[k] = (cos_a * cos_b - sin_a * sin_b, sin_a * cos_b + cos_a * sin_b)
                for s in range(2):
                    waves[k - 1, s, at:at + TILE, :] = powers[k][s]
                    part = fold(powers[k][s])
                    rows = pl.ds((s * knots + k - 1) * 8, 8)
                    for v in range(width // 128):
                        piece = part[:, v * 128:(v + 1) * 128]
                        acc[v, rows, :] = piece if first else acc[v, rows, :] + piece

    trig(0, project(0, core))
    wait_all(blocks.at[other], f_recv)
    trig(1, project(1, other))
    for v in range(width // 128):
        value = acc[v, pl.ds(0, 2 * knots, stride=8), :]
        for i in range(1, 8):
            value = value + acc[v, pl.ds(i, 2 * knots, stride=8), :]
        sums[b, :, v * 128:(v + 1) * 128] = value
    for a in batch_peers:
        remote(sums.at[b], sums.at[b], s_send, s_recv, (a, d)).start()

    knot = lax.broadcasted_iota(jnp.int32, (knots, width), 0).astype(jnp.float32) + 1.0
    pos = knot * SPACING
    target = jnp.exp(-0.5 * pos * pos)
    ends = jnp.where(knot == float(knots), 0.5, 1.0)
    weight = 2.0 * (ends * SPACING * target)
    wait_all(blocks.at[0], e_send)
    if chips > 1:
        wait_all(blocks.at[0, pl.ds(0, chips - 1)], f_send)
    if nb > 1:
        wait_all(sums.at[pl.ds(0, nb - 1)], s_recv)
    total = sums[0]
    for a in range(1, nb):
        total = total + sums[a]
    mean = total * (1.0 / total_rows)
    coef[0:knots, :] = pos * (weight * (mean[0:knots] - target))
    coef[knots:2 * knots, :] = pos * (weight * mean[knots:2 * knots])
    ones = jnp.full((1, width), 1.0, jnp.float32)
    zeros = jnp.zeros((1, width), jnp.float32)
    end = 2.0 * 0.5 * SPACING
    first_term = 0.0 * (ones * (end * zeros) - zeros * (end * (ones - 1.0)))

    for at in range(0, 2 * half, TILE):
        value = jnp.broadcast_to(first_term, (TILE, width))
        for k in range(knots):
            value = value + (
                waves[k, 0, at:at + TILE, :] * coef[knots + k:knots + k + 1, :]
                - waves[k, 1, at:at + TILE, :] * coef[k:k + 1, :]
            )
        grads[at:at + TILE, :] = value.astype(jnp.bfloat16)

    columns = depth // PARTS

    def back(value, p):
        return lax.dot_general(
            value, unit[p * columns:(p + 1) * columns, :], (((1,), (1,)), ((), ())),
            preferred_element_type=jnp.float32,
        )

    both = grads[...]
    for p in range(PARTS):
        value = back(both, p)
        kept[p] = value[0:half]
        pair_out[p] = value[half:2 * half]
        remote(pair_out.at[p], pair_in.at[p], p_send, p_recv.at[p], partner).start()
    for p in range(PARTS):
        wait_all(pair_in.at[p], p_recv.at[p])
        value = kept[p] + pair_in[p]
        for c in range(chips):
            z_own[p, c] = value[c * per:(c + 1) * per]
            z_out[p, c] = to_wire(value[c * per:(c + 1) * per])
        for c in chip_peers:
            remote(
                z_out.at[p, c], z_in.at[p, chip], z_send, z_recv.at[p], (b, c * 2 + core)
            ).start()
    if nb > 1:
        wait_all(sums.at[pl.ds(0, nb - 1)], s_send)
    wait_all(pair_out, p_send)
    for p in range(PARTS):
        value = z_own[p, chip]
        if chips > 1:
            wait_all(z_in.at[p, pl.ds(0, chips - 1)], z_recv.at[p])
        for c in chip_peers:
            value = value + from_wire(z_in[p, c])
        out_ref[:, p * columns:(p + 1) * columns] = value
    if chips > 1:
        wait_all(z_out.at[:, pl.ds(0, chips - 1)], z_send)


def local(nb, nd, embeddings, directions):
    per, depth = embeddings.shape
    width = directions.shape[1]
    chips = nd // 2
    half = chips * per
    knots = KNOTS - 1
    columns = depth // PARTS
    f32, bf16 = jnp.float32, jnp.bfloat16
    dma = pltpu.SemaphoreType.DMA
    return pl.pallas_call(
        functools.partial(kernel, nb, nd),
        out_shape=jax.ShapeDtypeStruct((per, depth), f32),
        in_specs=[pl.BlockSpec(memory_space=pltpu.HBM)] * 2,
        out_specs=pl.BlockSpec(memory_space=pltpu.VMEM),
        scratch_shapes=[
            pltpu.VMEM((depth, width), bf16),
            pltpu.VMEM((depth, width), bf16),
            pltpu.VMEM((2, chips, per, depth), bf16),
            pltpu.VMEM((half, depth), f32),
            pltpu.VMEM((knots, 2, 2 * half, width), f32),
            pltpu.VMEM((width // 128, 2 * knots * 8, 128), f32),
            pltpu.VMEM((nb, 2 * knots, width), f32),
            pltpu.VMEM((2 * knots, width), f32),
            pltpu.VMEM((2 * half, width), bf16),
            pltpu.VMEM((PARTS, half, columns), f32),
            pltpu.VMEM((PARTS, half, columns), f32),
            pltpu.VMEM((PARTS, half, columns), f32),
            pltpu.VMEM((PARTS, chips, per, columns), f32),
            pltpu.VMEM((PARTS, chips, per, columns), bf16),
            pltpu.VMEM((PARTS, chips, per, columns), bf16),
            dma,
            dma,
            dma,
            dma((chips,)),
            dma,
            dma,
            dma,
            dma,
            dma,
            dma((PARTS,)),
            dma,
            dma((PARTS,)),
        ],
        compiler_params=pltpu.CompilerParams(
            collective_id=0, has_side_effects=True, vmem_limit_bytes=56 * 1000 * 1000
        ),
        name="sigreg_backward",
    )(embeddings, directions)


def solution(mesh):
    placed = (P(("batch", "dir"), None), P(None, "dir"))
    return jax.shard_map(
        functools.partial(local, mesh.shape["batch"], mesh.shape["dir"]),
        mesh=mesh, in_specs=placed, out_specs=P(("batch", "dir"), None), check_vma=False,
    )
```

time: 23 us -> 21.6 us (0.939)
  Pallas kernels: 21.4 us -> 20 us
    pallas_call x1, Pallas kernels: 21.4 us -> 20 us  [local(): pl.pallas_call(functools.partial(kernel, nb, nd), out_shape=jax.ShapeDtyp...]
    unnamed x1 -> x3, local copies, waits for them, and re-layouts: 1.38 us -> 1.33 us
where the time goes in v7:
time: 21.6 us; the launch traced here: 21.3 us
  Pallas kernels  20 us (93%)
  local copies, waits for them, and re-layouts  1.33 us (6%)
    pallas_call x1, Pallas kernels, local(): pl.pallas_call(functools.partial(kernel, nb, nd), out_shape=jax.ShapeDtyp...  20 us
    unnamed x3, local copies, waits for them, and re-layouts  1.33 us

profile of v7, /device:TPU:0, one launch (start us, length us, event | category | flops | bytes accessed | tf_op | source)
XLA Modules:
  0.0 21.3 jit_solution(8802917447756629548)
XLA Ops:
  0.0 0.0 copy-start
  0.0 0.7 %copy-done = bf16[4,2048]{1,0:T(4,128)(2,1)S(1)} copy-done((bf16[4,2048]{1,0:T(4,128)(2,1)S(1)}, bf16[4,2048]{1,0:T(4,128)(2,1)}, u32[]{:S(2)}) %copy-start) | copy-done | bytes 16408
  0.7 20.0 %sigreg_backward.1 = f32[4,2048]{1,0:T(4,128)S(1)} custom-call(bf16[4,2048]{1,0:T(4,128)(2,1)S(1)} %copy-done, bf16[2048,256]{1,0:T(8,128)(2,1)} %dir_ref.1), custom_call_target="tpu_custom_call" | custom-call | tf_op jit(solution)/shard_map/sigreg_backward/pallas_call | solution.py:236
  20.7 0.6 %copy.4 = f32[4,2048]{1,0:T(4,128)} copy(f32[4,2048]{1,0:T(4,128)S(1)} %sigreg_backward.1) | data formatting | bytes 65536
Async XLA Ops:
  0.0 0.7 %copy-start = (bf16[4,2048]{1,0:T(4,128)(2,1)S(1)}, bf16[4,2048]{1,0:T(4,128)(2,1)}, u32[]{:S(2)}) copy-start(bf16[4,2048]{1,0:T(4,128)(2,1)} %emb_ref.1) | copy-start | bytes 49156

commit v8 on v7

--- a/solution.py
+++ b/solution.py
@@ -45,7 +45,7 @@
     nb, nd, emb_ref, dir_ref, out_ref,
     raw, unit, blocks, rows_f32, waves, acc, sums, coef, grads,
     kept, pair_out, pair_in, z_own, z_out, z_in,
-    raw_sem, own_sem, e_send, e_recv, f_send, f_recv, s_send, s_recv, p_send, p_recv, z_send, z_recv,
+    raw_sem, own_sem, up_send, down_send, e_recv, f_send, f_recv, s_send, s_recv, p_send, p_recv, z_send, z_recv,
 ):
     chips = nd // 2
     half = chips * emb_ref.shape[0]
@@ -75,18 +75,45 @@
     chip_peers = [lax.rem(chip + j, chips) for j in range(1, chips)]
     batch_peers = [lax.rem(b + j, nb) for j in range(1, nb)]
     barrier = pltpu.get_barrier_semaphore()
-    for c in chip_peers:
-        pl.semaphore_signal(barrier, inc=1, device_id=(b, c * 2 + core), device_id_type=MESH)
+    has_low, has_high = chip > 0, chip < chips - 1
+    low, high = (b, d - 2), (b, d + 2)
+
+    @pl.when(has_low)
+    def _():
+        pl.semaphore_signal(barrier, inc=1, device_id=low, device_id_type=MESH)
+
+    @pl.when(has_high)
+    def _():
+        pl.semaphore_signal(barrier, inc=1, device_id=high, device_id_type=MESH)
+
+    pl.semaphore_signal(barrier, inc=1, device_id=partner, device_id_type=MESH)
     for a in batch_peers:
         pl.semaphore_signal(barrier, inc=1, device_id=(a, d), device_id_type=MESH)
-    pl.semaphore_signal(barrier, inc=1, device_id=partner, device_id_type=MESH)
-    pl.semaphore_wait(barrier, len(chip_peers) + len(batch_peers) + 1)
-
-    mine = blocks.at[core, chip]
     own.wait()
-    for c in chip_peers:
-        remote(mine, mine, e_send, e_recv.at[chip], (b, c * 2 + core)).start()
-    remote(mine, mine, e_send, f_recv, partner).start()
+    neighbors = (chip + chips - 1) // chips + (2 * chips - 2 - chip) // chips
+    pl.semaphore_wait(barrier, len(batch_peers) + 1 + neighbors)
+
+    def go_up(c):
+        block = blocks.at[core, c]
+        return remote(block, block, up_send.at[c], e_recv.at[c], high)
+
+    def go_down(c):
+        block = blocks.at[core, c]
+        return remote(block, block, down_send.at[c], e_recv.at[c], low)
+
+    def go_across(c):
+        block = blocks.at[core, c]
+        return remote(block, block, f_send, f_recv, partner)
+
+    @pl.when(has_high)
+    def _():
+        go_up(chip).start()
+
+    @pl.when(has_low)
+    def _():
+        go_down(chip).start()
+
+    go_across(chip).start()
 
     load.wait()
     width = raw.shape[1]
@@ -99,6 +126,32 @@
     square = lax.fori_loop(0, STEPS, add_squares, jnp.zeros((8, width), jnp.float32))
     scale = 1.0 / jnp.sqrt(jnp.sum(square, axis=0, keepdims=True) + 1e-06)
 
+    def relay(step):
+        below, above = chip - step, chip + step
+
+        @pl.when(below >= 0)
+        def _():
+            go_up(below).wait_recv()
+
+            @pl.when(has_high)
+            def _():
+                go_up(below).start()
+
+            go_across(below).start()
+
+        @pl.when(above < chips)
+        def _():
+            go_down(above).wait_recv()
+
+            @pl.when(has_low)
+            def _():
+                go_down(above).start()
+
+            go_across(above).start()
+
+    if chips > 1:
+        relay(1)
+
     def normalize(i, carry):
         part = pl.ds(pl.multiple_of(i * step_rows, step_rows), step_rows)
         unit[part, :] = (raw[part, :].astype(jnp.float32) * scale).astype(jnp.bfloat16)
@@ -106,10 +159,8 @@
 
     lax.fori_loop(0, STEPS, normalize, 0)
 
-    for c in chip_peers:
-        block = blocks.at[core, c]
-        remote(block, block, f_send, e_recv.at[c], partner).wait_recv()
-        remote(block, block, f_send, f_recv, partner).start()
+    for step in range(2, chips):
+        relay(step)
 
     knots = KNOTS - 1
 
@@ -161,9 +212,18 @@
     target = jnp.exp(-0.5 * pos * pos)
     ends = jnp.where(knot == float(knots), 0.5, 1.0)
     weight = 2.0 * (ends * SPACING * target)
-    wait_all(blocks.at[0], e_send)
-    if chips > 1:
-        wait_all(blocks.at[0, pl.ds(0, chips - 1)], f_send)
+    for step in range(chips):
+        below, above = chip - step, chip + step
+
+        @pl.when((below >= 0) & has_high)
+        def _():
+            go_up(below).wait_send()
+
+        @pl.when((above < chips) & has_low)
+        def _():
+            go_down(above).wait_send()
+
+    wait_all(blocks.at[0], f_send)
     if nb > 1:
         wait_all(sums.at[pl.ds(0, nb - 1)], s_recv)
     total = sums[0]
@@ -256,7 +316,8 @@
             pltpu.VMEM((PARTS, chips, per, columns), bf16),
             dma,
             dma,
-            dma,
+            dma((chips,)),
+            dma((chips,)),
             dma((chips,)),
             dma,
             dma,

time: 21.6 us -> 23.9 us (1.11)
  Pallas kernels: 20 us -> 22.3 us
    pallas_call x1, Pallas kernels: 20 us -> 22.3 us  [local(): pl.pallas_call(functools.partial(kernel, nb, nd), out_shape=jax.ShapeDtyp...]
where the time goes in v8:
time: 23.9 us; the launch traced here: 23.7 us
  Pallas kernels  22.3 us (93%)
  local copies, waits for them, and re-layouts  1.33 us (6%)
    pallas_call x1, Pallas kernels, local(): pl.pallas_call(functools.partial(kernel, nb, nd), out_shape=jax.ShapeDtyp...  22.3 us
    unnamed x3, local copies, waits for them, and re-layouts  1.33 us

profile of v8, /device:TPU:0, one launch (start us, length us, event | category | flops | bytes accessed | tf_op | source)
XLA Modules:
  0.0 23.7 jit_solution(10689538869020168670)
XLA Ops:
  0.0 0.0 copy-start
  0.0 0.7 %copy-done = bf16[4,2048]{1,0:T(4,128)(2,1)S(1)} copy-done((bf16[4,2048]{1,0:T(4,128)(2,1)S(1)}, bf16[4,2048]{1,0:T(4,128)(2,1)}, u32[]{:S(2)}) %copy-start) | copy-done | bytes 16408
  0.7 22.3 %sigreg_backward.1 = f32[4,2048]{1,0:T(4,128)S(1)} custom-call(bf16[4,2048]{1,0:T(4,128)(2,1)S(1)} %copy-done, bf16[2048,256]{1,0:T(8,128)(2,1)} %dir_ref.1), custom_call_target="tpu_custom_call" | custom-call | tf_op jit(solution)/shard_map/sigreg_backward/pallas_call | solution.py:296
  23.0 0.6 %copy.4 = f32[4,2048]{1,0:T(4,128)} copy(f32[4,2048]{1,0:T(4,128)S(1)} %sigreg_backward.1) | data formatting | bytes 65536
Async XLA Ops:
  0.0 0.7 %copy-start = (bf16[4,2048]{1,0:T(4,128)(2,1)S(1)}, bf16[4,2048]{1,0:T(4,128)(2,1)}, u32[]{:S(2)}) copy-start(bf16[4,2048]{1,0:T(4,128)(2,1)} %emb_ref.1) | copy-start | bytes 49156

commit v9 on v7

--- a/solution.py
+++ b/solution.py
@@ -72,7 +72,12 @@
     own = pltpu.make_async_copy(emb_ref, blocks.at[core, chip], own_sem)
     own.start()
 
-    chip_peers = [lax.rem(chip + j, chips) for j in range(1, chips)]
+    upper = (2 * chip) // chips
+    near_end = upper * chip + (1 - upper) * (chips - 1 - chip)
+    chip_peers = []
+    for j in range(chips - 1):
+        c = j + (j + chips - near_end) // chips
+        chip_peers.append(upper * c + (1 - upper) * (chips - 1 - c))
     batch_peers = [lax.rem(b + j, nb) for j in range(1, nb)]
     barrier = pltpu.get_barrier_semaphore()
     for c in chip_peers:
@@ -106,7 +111,7 @@
 
     lax.fori_loop(0, STEPS, normalize, 0)
 
-    for c in chip_peers:
+    for c in reversed(chip_peers):
         block = blocks.at[core, c]
         remote(block, block, f_send, e_recv.at[c], partner).wait_recv()
         remote(block, block, f_send, f_recv, partner).start()

time: 21.6 us -> 21.3 us (0.986)
  Pallas kernels: 20 us -> 19.7 us
    pallas_call x1, Pallas kernels: 20 us -> 19.7 us  [local(): pl.pallas_call(functools.partial(kernel, nb, nd), out_shape=jax.ShapeDtyp...]
where the time goes in v9:
time: 21.3 us; the launch traced here: 21 us
  Pallas kernels  19.7 us (92%)
  local copies, waits for them, and re-layouts  1.33 us (6%)
    pallas_call x1, Pallas kernels, local(): pl.pallas_call(functools.partial(kernel, nb, nd), out_shape=jax.ShapeDtyp...  19.7 us
    unnamed x3, local copies, waits for them, and re-layouts  1.33 us

profile of v9, /device:TPU:0, one launch (start us, length us, event | category | flops | bytes accessed | tf_op | source)
XLA Modules:
  0.0 21.0 jit_solution(14534789121327658699)
XLA Ops:
  0.0 0.0 copy-start
  0.0 0.7 %copy-done = bf16[4,2048]{1,0:T(4,128)(2,1)S(1)} copy-done((bf16[4,2048]{1,0:T(4,128)(2,1)S(1)}, bf16[4,2048]{1,0:T(4,128)(2,1)}, u32[]{:S(2)}) %copy-start) | copy-done | bytes 16408
  0.7 19.7 %sigreg_backward.1 = f32[4,2048]{1,0:T(4,128)S(1)} custom-call(bf16[4,2048]{1,0:T(4,128)(2,1)S(1)} %copy-done, bf16[2048,256]{1,0:T(8,128)(2,1)} %dir_ref.1), custom_call_target="tpu_custom_call" | custom-call | tf_op jit(solution)/shard_map/sigreg_backward/pallas_call | solution.py:241
  20.4 0.6 %copy.4 = f32[4,2048]{1,0:T(4,128)} copy(f32[4,2048]{1,0:T(4,128)S(1)} %sigreg_backward.1) | data formatting | bytes 65536
Async XLA Ops:
  0.0 0.7 %copy-start = (bf16[4,2048]{1,0:T(4,128)(2,1)S(1)}, bf16[4,2048]{1,0:T(4,128)(2,1)}, u32[]{:S(2)}) copy-start(bf16[4,2048]{1,0:T(4,128)(2,1)} %emb_ref.1) | copy-start | bytes 49156

commit v10 on v9

--- a/solution.py
+++ b/solution.py
@@ -78,7 +78,11 @@
     for j in range(chips - 1):
         c = j + (j + chips - near_end) // chips
         chip_peers.append(upper * c + (1 - upper) * (chips - 1 - c))
-    batch_peers = [lax.rem(b + j, nb) for j in range(1, nb)]
+    mirror = nb - 1 - b
+    own_at = (b + nb - mirror) % nb
+    batch_peers = [
+        (mirror + j + (j + nb - own_at) // nb) % nb for j in range(nb - 1)
+    ]
     barrier = pltpu.get_barrier_semaphore()
     for c in chip_peers:
         pl.semaphore_signal(barrier, inc=1, device_id=(b, c * 2 + core), device_id_type=MESH)
@@ -118,7 +122,7 @@
 
     knots = KNOTS - 1
 
-    def project(which, side):
+    def project(side):
         for c in range(chips):
             rows_f32[c * per:(c + 1) * per, :] = blocks[side, c].astype(jnp.float32)
         return jnp.dot(
@@ -130,8 +134,7 @@
 
     def trig(which, projected):
         for r in range(half // TILE):
-            first = which == 0 and r == 0
-            at = which * half + r * TILE
+            at = r * TILE
             sine1, cosine1 = sin_cos(SPACING * projected[r * TILE:(r + 1) * TILE])
             powers = {1: (cosine1, sine1)}
             for k in range(1, KNOTS):
@@ -143,16 +146,24 @@
                     (cos_a, sin_a), (cos_b, sin_b) = powers[k // 2], powers[k // 2 + 1]
                     powers[k] = (cos_a * cos_b - sin_a * sin_b, sin_a * cos_b + cos_a * sin_b)
                 for s in range(2):
-                    waves[k - 1, s, at:at + TILE, :] = powers[k][s]
+                    waves[k - 1, s, which, at:at + TILE, :] = powers[k][s]
                     part = fold(powers[k][s])
                     rows = pl.ds((s * knots + k - 1) * 8, 8)
                     for v in range(width // 128):
                         piece = part[:, v * 128:(v + 1) * 128]
-                        acc[v, rows, :] = piece if first else acc[v, rows, :] + piece
-
-    trig(0, project(0, core))
-    wait_all(blocks.at[other], f_recv)
-    trig(1, project(1, other))
+                        acc[v, rows, :] += piece
+
+    acc[...] = jnp.zeros_like(acc)
+
+    def stage(which, carry):
+        @pl.when(which == 1)
+        def _():
+            wait_all(blocks.at[other], f_recv)
+
+        trig(which, project(lax.rem(core + which, 2)))
+        return carry
+
+    lax.fori_loop(0, 2, stage, 0)
     for v in range(width // 128):
         value = acc[v, pl.ds(0, 2 * knots, stride=8), :]
         for i in range(1, 8):
@@ -182,12 +193,14 @@
     end = 2.0 * 0.5 * SPACING
     first_term = 0.0 * (ones * (end * zeros) - zeros * (end * (ones - 1.0)))
 
-    for at in range(0, 2 * half, TILE):
+    for tile in range(2 * half // TILE):
+        at = tile * TILE
+        which, start = at // half, at % half
         value = jnp.broadcast_to(first_term, (TILE, width))
         for k in range(knots):
             value = value + (
-                waves[k, 0, at:at + TILE, :] * coef[knots + k:knots + k + 1, :]
-                - waves[k, 1, at:at + TILE, :] * coef[k:k + 1, :]
+                waves[k, 0, which, start:start + TILE, :] * coef[knots + k:knots + k + 1, :]
+                - waves[k, 1, which, start:start + TILE, :] * coef[k:k + 1, :]
             )
         grads[at:at + TILE, :] = value.astype(jnp.bfloat16)
 
@@ -195,16 +208,20 @@
 
     def back(value, p):
         return lax.dot_general(
-            value, unit[p * columns:(p + 1) * columns, :], (((1,), (1,)), ((), ())),
+            value, unit[pl.ds(pl.multiple_of(p * columns, columns), columns), :], (((1,), (1,)), ((), ())),
             preferred_element_type=jnp.float32,
         )
 
     both = grads[...]
-    for p in range(PARTS):
+
+    def back_part(p, carry):
         value = back(both, p)
         kept[p] = value[0:half]
         pair_out[p] = value[half:2 * half]
         remote(pair_out.at[p], pair_in.at[p], p_send, p_recv.at[p], partner).start()
+        return carry
+
+    lax.fori_loop(0, PARTS, back_part, 0)
     for p in range(PARTS):
         wait_all(pair_in.at[p], p_recv.at[p])
         value = kept[p] + pair_in[p]
@@ -248,7 +265,7 @@
             pltpu.VMEM((depth, width), bf16),
             pltpu.VMEM((2, chips, per, depth), bf16),
             pltpu.VMEM((half, depth), f32),
-            pltpu.VMEM((knots, 2, 2 * half, width), f32),
+            pltpu.VMEM((knots, 2, 2, half, width), f32),
             pltpu.VMEM((width // 128, 2 * knots * 8, 128), f32),
             pltpu.VMEM((nb, 2 * knots, width), f32),
             pltpu.VMEM((2 * knots, width), f32),

time: 21.3 us -> 21 us (0.986)
    pallas_call x1, Pallas kernels: 19.7 us -> 19.5 us  [local(): pl.pallas_call(functools.partial(kernel, nb, nd), out_shape=jax.ShapeDtyp...]
where the time goes in v10:
time: 21 us; the launch traced here: 20.8 us
  Pallas kernels  19.5 us (93%)
  local copies, waits for them, and re-layouts  1.33 us (6%)
    pallas_call x1, Pallas kernels, local(): pl.pallas_call(functools.partial(kernel, nb, nd), out_shape=jax.ShapeDtyp...  19.5 us
    unnamed x3, local copies, waits for them, and re-layouts  1.33 us

profile of v10, /device:TPU:0, one launch (start us, length us, event | category | flops | bytes accessed | tf_op | source)
XLA Modules:
  0.0 20.8 jit_solution(4346121639368436198)
XLA Ops:
  0.0 0.0 copy-start
  0.0 0.7 %copy-done = bf16[4,2048]{1,0:T(4,128)(2,1)S(1)} copy-done((bf16[4,2048]{1,0:T(4,128)(2,1)S(1)}, bf16[4,2048]{1,0:T(4,128)(2,1)}, u32[]{:S(2)}) %copy-start) | copy-done | bytes 16408
  0.7 19.5 %sigreg_backward.1 = f32[4,2048]{1,0:T(4,128)S(1)} custom-call(bf16[4,2048]{1,0:T(4,128)(2,1)S(1)} %copy-done, bf16[2048,256]{1,0:T(8,128)(2,1)} %dir_ref.1), custom_call_target="tpu_custom_call" | custom-call | tf_op jit(solution)/shard_map/sigreg_backward/pallas_call | solution.py:258
  20.2 0.6 %copy.4 = f32[4,2048]{1,0:T(4,128)} copy(f32[4,2048]{1,0:T(4,128)S(1)} %sigreg_backward.1) | data formatting | bytes 65536
Async XLA Ops:
  0.0 0.7 %copy-start = (bf16[4,2048]{1,0:T(4,128)(2,1)S(1)}, bf16[4,2048]{1,0:T(4,128)(2,1)}, u32[]{:S(2)}) copy-start(bf16[4,2048]{1,0:T(4,128)(2,1)} %emb_ref.1) | copy-start | bytes 49156

commit v11 on v10

--- a/solution.py
+++ b/solution.py
@@ -293,7 +293,10 @@
             collective_id=0, has_side_effects=True, vmem_limit_bytes=56 * 1000 * 1000
         ),
         name="sigreg_backward",
-    )(embeddings, directions)
+    )(
+        pltpu.with_memory_space_constraint(embeddings, pltpu.HBM),
+        pltpu.with_memory_space_constraint(directions, pltpu.HBM),
+    )
 
 
 def solution(mesh):

time: 21 us -> 20.2 us (0.962)
  local copies, waits for them, and re-layouts: 1.33 us -> 0.62 us
    unnamed x3 -> x1, local copies, waits for them, and re-layouts: 1.33 us -> 0.62 us
where the time goes in v11:
time: 20.2 us; the launch traced here: 20.1 us
  Pallas kernels  19.5 us (97%)
  local copies, waits for them, and re-layouts  0.62 us (3%)
    pallas_call x1, Pallas kernels, local(): pl.pallas_call(functools.partial(kernel, nb, nd), out_shape=jax.ShapeDtyp...  19.5 us
    unnamed x1, local copies, waits for them, and re-layouts  0.62 us

profile of v11, /device:TPU:0, one launch (start us, length us, event | category | flops | bytes accessed | tf_op | source)
XLA Modules:
  0.0 20.1 jit_solution(3169760837871568853)
XLA Ops:
  0.0 19.5 %sigreg_backward.1 = f32[4,2048]{1,0:T(4,128)S(1)} custom-call(bf16[4,2048]{1,0:T(4,128)(2,1)} %emb_ref.1, bf16[2048,256]{1,0:T(8,128)(2,1)} %dir_ref.1), custom_call_target="tpu_custom_call" | custom-call | tf_op jit(solution)/shard_map/sigreg_backward/pallas_call | solution.py:258
  19.5 0.6 %copy.4 = f32[4,2048]{1,0:T(4,128)} copy(f32[4,2048]{1,0:T(4,128)S(1)} %sigreg_backward.1) | data formatting | bytes 65536

commit v12 on v11

--- a/solution.py
+++ b/solution.py
@@ -67,8 +67,6 @@
     def wait_all(ref, sem):
         pltpu.make_async_copy(ref, ref, sem).wait()
 
-    load = pltpu.make_async_copy(dir_ref, raw, raw_sem)
-    load.start()
     own = pltpu.make_async_copy(emb_ref, blocks.at[core, chip], own_sem)
     own.start()
 
@@ -89,6 +87,8 @@
     for a in batch_peers:
         pl.semaphore_signal(barrier, inc=1, device_id=(a, d), device_id_type=MESH)
     pl.semaphore_signal(barrier, inc=1, device_id=partner, device_id_type=MESH)
+    load = pltpu.make_async_copy(dir_ref, raw, raw_sem)
+    load.start()
     pl.semaphore_wait(barrier, len(chip_peers) + len(batch_peers) + 1)
 
     mine = blocks.at[core, chip]

time: 20.2 us -> 20.2 us (level)
  no operation moved by 1% of the time
where the time goes in v12:
time: 20.2 us; the launch traced here: 20.1 us
  Pallas kernels  19.5 us (97%)
  local copies, waits for them, and re-layouts  0.62 us (3%)
    pallas_call x1, Pallas kernels, local(): pl.pallas_call(functools.partial(kernel, nb, nd), out_shape=jax.ShapeDtyp...  19.5 us
    unnamed x1, local copies, waits for them, and re-layouts  0.62 us

profile of v12, /device:TPU:0, one launch (start us, length us, event | category | flops | bytes accessed | tf_op | source)
XLA Modules:
  0.0 20.1 jit_solution(16019137832384083237)
XLA Ops:
  0.0 19.5 %sigreg_backward.1 = f32[4,2048]{1,0:T(4,128)S(1)} custom-call(bf16[4,2048]{1,0:T(4,128)(2,1)} %emb_ref.1, bf16[2048,256]{1,0:T(8,128)(2,1)} %dir_ref.1), custom_call_target="tpu_custom_call" | custom-call | tf_op jit(solution)/shard_map/sigreg_backward/pallas_call | solution.py:258
  19.5 0.6 %copy.4 = f32[4,2048]{1,0:T(4,128)} copy(f32[4,2048]{1,0:T(4,128)S(1)} %sigreg_backward.1) | data formatting | bytes 65536

commit v13 on v12

--- a/solution.py
+++ b/solution.py
@@ -11,7 +11,7 @@
 SPACING = 3.0 / (KNOTS - 1)
 MESH = pl.DeviceIdType.MESH
 TILE = 16
-PARTS = 2
+PARTS = 4
 STEPS = 8
 LIFT = 2.0 ** 50
 

time: 20.2 us -> 20.3 us (level)
  no operation moved by 1% of the time
where the time goes in v13:
time: 20.3 us; the launch traced here: 20.1 us
  Pallas kernels  19.5 us (96%)
  local copies, waits for them, and re-layouts  0.62 us (3%)
    pallas_call x1, Pallas kernels, local(): pl.pallas_call(functools.partial(kernel, nb, nd), out_shape=jax.ShapeDtyp...  19.5 us
    unnamed x1, local copies, waits for them, and re-layouts  0.62 us

profile of v13, /device:TPU:0, one launch (start us, length us, event | category | flops | bytes accessed | tf_op | source)
XLA Modules:
  0.0 20.1 jit_solution(8960950769739701020)
XLA Ops:
  0.0 19.5 %sigreg_backward.1 = f32[4,2048]{1,0:T(4,128)S(1)} custom-call(bf16[4,2048]{1,0:T(4,128)(2,1)} %emb_ref.1, bf16[2048,256]{1,0:T(8,128)(2,1)} %dir_ref.1), custom_call_target="tpu_custom_call" | custom-call | tf_op jit(solution)/shard_map/sigreg_backward/pallas_call | solution.py:258
  19.5 0.6 %copy.4 = f32[4,2048]{1,0:T(4,128)} copy(f32[4,2048]{1,0:T(4,128)S(1)} %sigreg_backward.1) | data formatting | bytes 65536
